TPU v7x, 256 devices: a whole 4x4x8 slice. The times are simulated.
256 devices in a mesh: row: 16 (over x, z_hi), col: 16 (over z_lo, y, core).
Axes of the slice: x: 4, y: 4, z: 8 (z_hi: 4, z_lo: 2; z = z_hi * 2 + z_lo), core: 2. Of those that a mesh axis runs over, the one named last changes fastest.
Arguments:
- observed: float32 [65536, 128], P('row'), may hold values from -6 to 6
- slip: float32 [32768, 256], P('col'), may hold values from 0 to 1.5
- green_left: bfloat16 [65536, 2048], P('row', 'col'), may hold values from -0.5 to 0.5
- green_right: bfloat16 [32768, 4096], P('col', 'row'), may hold values from -0.0234375 to 0.0234375
- block_ranks: int32 [16, 16], P('row', 'col'), may hold values from 32 to 128
- neighbours: int32 [32768, 8], P('col'), may hold values from 0 to 32767, as said below
Outputs:
- slip_next: float32 [32768, 256], P('col')
- residual: float32 [65536, 128], P('row')
Inputs may be any that keep to these rules, and one draw needn't show every extreme that they name: `neighbours`: each entry lies within 64 patch numbers of its own patch; an entry equal to the patch itself is padding.
All inputs are finite; a program needn't handle non-finite values.
Results may differ from a plain program's by a relative error of at most 0.0037.
Values sent between devices are 32-bit elements; how exact they have to be, the bound alone decides.
A program may use at most 128 MiB of HBM per device.

v0:
```python
import jax
import jax.numpy as jnp
from jax import lax
from jax.sharding import PartitionSpec as P

HALO = 64


def padded(block, sides, width):
    for axis, dim in sides:
        count = lax.axis_size(axis)
        forward = [(i, i + 1) for i in range(count - 1)]
        backward = [(target, source) for source, target in forward]
        low = lax.ppermute(
            lax.slice_in_dim(block, block.shape[dim] - width, None, axis=dim), axis, forward
        )
        high = lax.ppermute(lax.slice_in_dim(block, 0, width, axis=dim), axis, backward)
        block = jnp.concatenate([low, block, high], axis=dim)
    return block


def body(observed, slip, green_left, green_right, block_ranks, neighbours):
    rows, kmax = green_left.shape
    patches = slip.shape[0]
    nrhs = slip.shape[1] // 2
    keep = (jnp.arange(kmax, dtype=jnp.int32) < block_ranks[0, 0]).astype(jnp.float32)[:, None]
    right_view = green_right.reshape(patches, 2, kmax)
    slip_half = slip.astype(jnp.bfloat16).reshape(patches, 2, nrhs)
    inner = jnp.einsum("pak,pan->kn", right_view, slip_half, preferred_element_type=jnp.float32)
    inner_half = (inner * keep).astype(jnp.bfloat16)
    predicted = jnp.dot(green_left, inner_half, preferred_element_type=jnp.float32)
    residual = lax.psum(predicted, "col") - observed
    extended = padded(slip, (("col", 0),), HALO)
    offset = lax.axis_index("col") * patches - HALO
    local_index = neighbours - offset
    smooth = 8.0 * slip
    for index in range(8):
        smooth = smooth - jnp.take(extended, local_index[:, index], axis=0)
    res_half = residual.astype(jnp.bfloat16)
    back = jnp.einsum("ik,in->kn", green_left, res_half, preferred_element_type=jnp.float32)
    back_half = (back * keep).astype(jnp.bfloat16)
    partial_value = jnp.einsum(
        "pak,kn->pan", right_view, back_half, preferred_element_type=jnp.float32
    )
    gradient = lax.psum(partial_value.reshape(patches, 2 * nrhs), "row")
    slip_next = jnp.maximum(slip - 0.5 * (gradient + 0.05 * smooth), 0.0)
    return (slip_next, residual)


def solution(mesh):
    return jax.shard_map(
        body,
        mesh=mesh,
        in_specs=(
            P("row", None),
            P("col", None),
            P("row", "col"),
            P("col", "row"),
            P("row", "col"),
            P("col", None),
        ),
        out_specs=(P("col", None), P("row", None)),
        check_vma=False,
    )
```

profile of v0, /device:TPU:2, one launch (start us, length us, event | category | flops | bytes accessed | tf_op | source)
XLA Modules:
  0.0 356.0 jit_solution(4145432588217758023)
XLA Ops:
  7.2 0.0 copy-start
  7.2 0.0 all-reduce.3.cloned.1.call-start
  7.2 1.0 fusion.33
  8.2 1.7 collective-permute-start
  10.6 0.2 collective-permute-done
  10.8 3.5 constant_dynamic-update-slice_fusion.1
  14.3 0.0 copy-done
  14.3 3.8 %convolution_bitcast_fusion = f32[4096,128]{0,1:T(8,128)} fusion(bf16[4096,128]{1,0:T(8,128)(2,1)S(1)} %copy-done, bf16[256,2,8,128]{3,2,1,0:T(8,128)(2,1)} %get-tuple-element.8, f32[128]{0:T(128)S(1)} %compare_convert_fusion, bf16[2048,256]{1,0:T(8,128)(2,1)} %param.11), kind=kOutput, calls=%fused_computation.8 | convolution fusion | flops 268468224 | bytes 5243392 | tf_op jit(solution)/shard_map/dot_general | solution.py:31
  18.1 0.0 all-reduce.3.cloned.1.call-update
  18.1 0.0 all-reduce.5.cloned.1.call-start
  18.1 1.3 collective-permute-start.1
  19.5 0.0 copy-start.2
  19.5 2.9 copy.8
  22.4 0.0 copy-done.2
  22.4 129.4 %all-reduce.3.cloned.1.call-done = f32[4096,128]{0,1:T(8,128)} async-done(((f32[4096,128]{0,1:T(8,128)}), f32[4096,128]{0,1:T(8,128)}) %all-reduce.3.cloned.1.call-update) | async-done | bytes 2097168 | tf_op jit(solution)/shard_map/psum | solution.py:32
  151.7 3.8 %sub.39 = f32[4096,128]{0,1:T(8,128)} subtract(f32[4096,128]{0,1:T(8,128)} %all-reduce.3.cloned.1.call-done, f32[4096,128]{0,1:T(8,128)} %copy.8) | non-fusion elementwise | flops 524288 | bytes 6291456 | tf_op jit(solution)/shard_map/sub | solution.py:32
  155.6 4.0 %fusion.15 = f32[128,2048,2]{1,0,2:T(8,128)} fusion(bf16[4096,128]{1,0:T(8,128)(2,1)S(1)} %copy-done, f32[4096,128]{0,1:T(8,128)} %sub.39, f32[128]{0:T(128)S(1)} %compare_convert_fusion, bf16[2048,256]{1,0:T(8,128)(2,1)} %param.11), kind=kOutput, calls=%fused_computation.31 | convolution fusion | flops 268992512 | bytes 6291968 | tf_op jit(solution)/shard_map/pak,kn->pan/dot_general | solution.py:42
  159.5 2.9 copy.10
  162.5 0.0 all-reduce.5.cloned.1.call-update
  162.7 0.0 collective-permute-done.1
  162.7 8.6 %gather_fusion.2 = f32[2048,256]{1,0:T(8,128)} fusion(f32[2176,256]{1,0:T(8,128)S(1)} %constant_dynamic-update-slice_fusion, s32[2048]{0:T(1024)S(1)} %get-tuple-element.19), kind=kCustom, calls=%fused_computation.2.clone | custom fusion | bytes 4202496 | tf_op jit(solution)/shard_map/jit(_take)/gather | solution.py:38
  171.3 8.6 %gather_fusion.3 = f32[2048,256]{1,0:T(8,128)} fusion(f32[2176,256]{1,0:T(8,128)S(1)} %constant_dynamic-update-slice_fusion, s32[2048]{0:T(1024)S(1)} %get-tuple-element.20), kind=kCustom, calls=%fused_computation.3.clone | custom fusion | bytes 4202496 | tf_op jit(solution)/shard_map/jit(_take)/gather | solution.py:38
  179.9 8.6 %gather_fusion.4 = f32[2048,256]{1,0:T(8,128)} fusion(f32[2176,256]{1,0:T(8,128)S(1)} %constant_dynamic-update-slice_fusion, s32[2048]{0:T(1024)S(1)} %get-tuple-element.21), kind=kCustom, calls=%fused_computation.4.clone | custom fusion | bytes 4202496 | tf_op jit(solution)/shard_map/jit(_take)/gather | solution.py:38
  188.4 8.6 %gather_fusion.5 = f32[2048,256]{1,0:T(8,128)} fusion(f32[2176,256]{1,0:T(8,128)S(1)} %constant_dynamic-update-slice_fusion, s32[2048]{0:T(1024)S(1)} %get-tuple-element.22), kind=kCustom, calls=%fused_computation.5.clone | custom fusion | bytes 4202496 | tf_op jit(solution)/shard_map/jit(_take)/gather | solution.py:38
  197.0 8.6 %gather_fusion.6 = f32[2048,256]{1,0:T(8,128)} fusion(f32[2176,256]{1,0:T(8,128)S(1)} %constant_dynamic-update-slice_fusion, s32[2048]{0:T(1024)S(1)} %get-tuple-element.23), kind=kCustom, calls=%fused_computation.6.clone | custom fusion | bytes 4202496 | tf_op jit(solution)/shard_map/jit(_take)/gather | solution.py:38
  205.6 8.6 %gather_fusion.7 = f32[2048,256]{1,0:T(8,128)} fusion(f32[2176,256]{1,0:T(8,128)S(1)} %constant_dynamic-update-slice_fusion, s32[2048]{0:T(1024)S(1)} %get-tuple-element.24), kind=kCustom, calls=%fused_computation.7.clone | custom fusion | bytes 4202496 | tf_op jit(solution)/shard_map/jit(_take)/gather | solution.py:38
  214.2 8.6 %gather_fusion = f32[2048,256]{1,0:T(8,128)} fusion(f32[2176,256]{1,0:T(8,128)S(1)} %constant_dynamic-update-slice_fusion, s32[2048]{0:T(1024)S(1)} %get-tuple-element.17), kind=kCustom, calls=%fused_computation.clone | custom fusion | bytes 4202496 | tf_op jit(solution)/shard_map/jit(_take)/gather | solution.py:38
  222.8 8.6 %gather_fusion.1 = f32[2048,256]{1,0:T(8,128)} fusion(f32[2176,256]{1,0:T(8,128)S(1)} %constant_dynamic-update-slice_fusion, s32[2048]{0:T(1024)S(1)} %get-tuple-element.18), kind=kCustom, calls=%fused_computation.1.clone | custom fusion | bytes 4202496 | tf_op jit(solution)/shard_map/jit(_take)/gather | solution.py:38
  231.4 3.0 copy.11
  234.4 104.5 %all-reduce.5.cloned.1.call-done = f32[2048,256]{1,0:T(8,128)} async-done(((f32[2048,256]{1,0:T(8,128)}), f32[2048,256]{1,0:T(8,128)}) %all-reduce.5.cloned.1.call-update) | async-done | bytes 2097168 | tf_op jit(solution)/shard_map/psum | solution.py:45
  338.9 0.0 copy-done.1
  338.9 10.3 %fusion.4 = f32[2048,256]{1,0:T(8,128)} fusion(f32[2048,256]{1,0:T(8,128)S(1)} %copy-done.1, f32[2048,256]{1,0:T(8,128)} %all-reduce.5.cloned.1.call-done, f32[2048,256]{1,0:T(8,128)} %gather_fusion.7, f32[2048,256]{1,0:T(8,128)} %gather_fusion.6, f32[2048,256]{1,0:T(8,128)} %gather_fusion.5, f32[2048,256]{1,0:T(8,128)} %gather_fusion.4, ...), kind=kLoop, calls=%fused_computation.14 | loop fusion | flops 11534336 | bytes 23085056 | tf_op jit(solution)/shard_map/max | solution.py:46
  (14 shorter events, 0.1 us)
Async XLA Ops:
  7.2 7.1 %copy-start = (bf16[4096,128]{1,0:T(8,128)(2,1)S(1)}, bf16[4096,128]{1,0:T(8,128)(2,1)}, u32[]{:S(2)}) copy-start(bf16[4096,128]{1,0:T(8,128)(2,1)} %param.10) | copy-start | bytes 3145732
  7.2 144.6 %all-reduce.3.cloned.1.call-start = ((), (), s32[]{:S(2)}) async-start(), calls=%async_computation | async-start | bytes 4194304 | tf_op jit(solution)/shard_map/psum | solution.py:32
  8.2 2.6 collective-permute-start
  18.1 320.8 %all-reduce.5.cloned.1.call-start = ((), (), s32[]{:S(2)}) async-start(), calls=%async_computation.1 | async-start | bytes 4194304 | tf_op jit(solution)/shard_map/psum | solution.py:45
  18.1 144.5 %collective-permute-start.1 = (f32[64,256]{1,0:T(8,128)S(1)}, f32[64,256]{1,0:T(8,128)S(1)}, u32[]{:S(2)}, u32[]{:S(2)}) collective-permute-start(f32[64,256]{1,0:T(8,128)S(1)} %get-tuple-element.5), channel_id=1, source_target_pairs={{1,0},{2,1},{3,2},{4,3},{5,4},{6,5},{7,6},{8,7},{9,8},{10,9},{11,1... | collective-permute-start | bytes 196616 | tf_op jit(solution)/shard_map/ppermute | solution.py:17
  19.5 2.9 copy-start.2
  231.4 107.5 %copy-start.1 = (f32[2048,256]{1,0:T(8,128)S(1)}, f32[2048,256]{1,0:T(8,128)}, u32[]{:S(2)}) copy-start(f32[2048,256]{1,0:T(8,128)} %param.9) | copy-start | bytes 6291460
Sparse Core Ops, SparseCore 0:
  18.2 133.4 all-reduce.2
  162.6 176.2 all-reduce.4
where the time goes:
time: 362 us; the launch traced here: 356 us
  waiting for transfers between devices  234 us (65%)
  local copies, waits for them, and re-layouts  78.6 us (22%)
  other arithmetic  17.6 us (5%)
  between operations  14.8 us (4%)
  matrix products  7.77 us (2%)
    psum x1, waiting for transfers between devices, body(): residual = lax.psum(predicted, 'col') - observed  129 us
    psum x1, waiting for transfers between devices, body(): gradient = lax.psum(partial_value.reshape(patches, 2 * nrhs), 'row')  104 us
    gather x8, local copies, waits for them, and re-layouts, body(): smooth = smooth - jnp.take(extended, local_index[:, index], axis=0)  68.7 us
    max x1, other arithmetic, body(): slip_next = jnp.maximum(slip - 0.5 * (gradient + 0.05 * smooth), 0.0)  10.3 us
  transfers between devices with their start and end apart: 4, of which 3 were waited for; matrix products, arithmetic and copies ran while one was open for 24% of the time, Pallas kernels for 0%

commit v1 on v0

v1 whole, which is shorter than its diff:
```python
import jax
import jax.numpy as jnp
from jax import lax
from jax.experimental import pallas as pl
from jax.experimental.pallas import tpu as pltpu
from jax.sharding import PartitionSpec as P

MESH = pl.DeviceIdType.MESH
F32 = jnp.float32
BF16 = jnp.bfloat16
HALO = 64
N_SEM = 160


def lane_low(shape):
    return lax.broadcasted_iota(jnp.int32, shape, 1) < 64


def swap_lanes(value):
    return pltpu.roll(value, 64, 1)


def ds(start, size, unit):
    if isinstance(start, int):
        return pl.ds(start, size)
    return pl.ds(pl.multiple_of(start, unit), size)


def kernel(
    obs, slip, gl, gr, rank, nbr, out, res,
    ext, glv, grv, obsv, nbrv, glsend, glrecv, xy, xyt, grsend, grrecv, grcat,
    insend, inrecv, rhs, pred, am1, ar, am3, zs, zr, resp, bsend, brecv, bx, bd, grad,
    cm1, cr, cm3, base, outp, outv, resv, send_sem, recv_sem, local_sem,
):
    row = lax.axis_index("row")
    col = lax.axis_index("col")
    x, zh = row // 4, row % 4
    zl, y, k = col // 8, (col // 2) % 4, col % 2

    def device(x, zh, zl, y, k):
        return (x * 4 + zh, (zl * 4 + y) * 2 + k)

    sibling = device(x, zh, zl, y, 1 - k)
    y_next = device(x, zh, zl, (y + 1) % 4, k)
    y_prev = device(x, zh, zl, (y + 3) % 4, k)
    z_pair = device(x, zh, 1 - zl, y, k)
    x_next = device((x + 1) % 4, zh, zl, y, k)
    x_prev = device((x + 3) % 4, zh, zl, y, k)
    x_far = device((x + 2) % 4, zh, zl, y, k)
    zh_next = device(x, (zh + 1) % 4, zl, y, k)
    zh_prev = device(x, (zh + 3) % 4, zl, y, k)
    col_next = (row, (col + 1) % 16)
    col_prev = (row, (col + 15) % 16)
    partners = (
        sibling, y_next, y_prev, z_pair, x_next, x_prev, x_far, zh_next, zh_prev, col_next, col_prev,
    )

    counts = [0, 0]
    sends = []

    def send(src, dst, to):
        index = counts[0]
        counts[0] += 1
        copy = pltpu.make_async_remote_copy(
            src_ref=src, dst_ref=dst, send_sem=send_sem.at[index], recv_sem=recv_sem.at[index],
            device_id=to, device_id_type=MESH,
        )
        copy.start()
        sends.append(copy)
        return copy

    def local(src, dst):
        index = counts[1]
        counts[1] += 1
        copy = pltpu.make_async_copy(src, dst, local_sem.at[index])
        copy.start()
        return copy

    load_gl = [
        local(gl.at[ds((1 - k) * 2048, 2048, 2048)], glv.at[pl.ds(2048, 2048)]),
    ]
    load_gr, load_slip = [], []
    for piece in range(4):
        rows = pl.ds(piece * 512, 512)
        load_gr.append(local(gr.at[rows], grv.at[rows]))
        load_slip.append(local(slip.at[rows], ext.at[pl.ds(HALO + piece * 512, 512)]))
    load_gl.append(local(gl.at[ds(k * 2048, 2048, 2048)], glv.at[pl.ds(0, 2048)]))
    shard = y * 256 + zl * 128
    load_obs = [
        local(obs.at[ds(k * 2048 + half * 1024 + shard, 128, 128)], obsv.at[half]) for half in range(2)
    ]
    load_nbr = local(nbr.at[:, ds(row * 128, 128, 128)], nbrv)

    barrier = pltpu.get_barrier_semaphore()
    for partner in partners:
        pl.semaphore_signal(barrier, inc=1, device_id=partner, device_id_type=MESH)

    load_gl[0].wait()

    def widen_left(i, carry):
        rows = ds(i * 256, 256, 256)
        glsend[rows, :] = glv[ds(2048 + i * 256, 256, 256), :].astype(F32)
        return carry

    lax.fori_loop(0, 8, widen_left, 0)
    pl.semaphore_wait(barrier, len(partners))
    swap_gl = [send(glsend.at[pl.ds(i * 512, 512)], glrecv.at[pl.ds(i * 512, 512)], sibling) for i in range(4)]

    keep = lax.broadcasted_iota(jnp.int32, (128, 128), 0) < rank[0, 0]

    inner = jnp.zeros((128, 128), F32)
    for piece in range(4):
        load_gr[piece].wait()
        load_slip[piece].wait()
        for rake in range(2):
            lanes = pl.ds(rake * 128, 128)
            inner += lax.dot_general(
                grv[pl.ds(piece * 512, 512), lanes],
                ext[pl.ds(HALO + piece * 512, 512), lanes].astype(BF16),
                (((0,), (0,)), ((), ())),
                preferred_element_type=F32,
            )
    inner = jnp.where(keep, inner, 0.0).astype(BF16).astype(F32)
    insend[...] = inner
    swap_inner = send(insend, inrecv, sibling)

    def widen_right(i, carry):
        rows = ds(i * 256, 256, 256)
        grsend[rows, :] = grv[rows, :].astype(F32)
        return carry

    lax.fori_loop(0, 8, widen_right, 0)

    def x_block(at):
        return ds(((x + at) % 4) * 512, 512, 512)

    share_gr = [
        send(grsend.at[x_block(3)], grrecv.at[0], x_prev),
        send(grsend.at[x_block(2)], grrecv.at[1], x_far),
        send(grsend.at[x_block(1)], grrecv.at[2], x_next),
    ]
    halo = [
        send(ext.at[pl.ds(2048, HALO)], ext.at[pl.ds(0, HALO)], col_next),
        send(ext.at[pl.ds(HALO, HALO)], ext.at[pl.ds(2048 + HALO, HALO)], col_prev),
    ]

    load_gl[1].wait()

    def own_left(i, carry):
        rows = ds(i * 256, 256, 256)
        xy[rows, pl.ds(0, 128)] = glv[rows, :]
        xy[rows, pl.ds(256, 128)] = glv[ds(1024 + i * 256, 256, 256), :]
        return carry

    lax.fori_loop(0, 4, own_left, 0)
    for copy in swap_gl:
        copy.wait_recv()

    def other_left(i, carry):
        rows = ds(i * 256, 256, 256)
        xy[rows, pl.ds(128, 128)] = glrecv[rows, :].astype(BF16)
        xy[rows, pl.ds(384, 128)] = glrecv[ds(1024 + i * 256, 256, 256), :].astype(BF16)
        return carry

    lax.fori_loop(0, 4, other_left, 0)
    for copy in load_obs:
        copy.wait()
    swap_inner.wait_recv()
    low = lane_low((256, 128))
    both = jnp.concatenate([inner, inrecv[...]], axis=0)
    turned = swap_lanes(both)
    rhs[0, pl.ds(0, 256), :] = jnp.where(low, both, 0.0).astype(BF16)
    rhs[0, pl.ds(256, 256), :] = jnp.where(low, 0.0, turned).astype(BF16)
    rhs[1, pl.ds(0, 256), :] = jnp.where(low, turned, 0.0).astype(BF16)
    rhs[1, pl.ds(256, 256), :] = jnp.where(low, 0.0, both).astype(BF16)

    def chain(h):
        values = pred.at[h]

        def predict(i, carry):
            rows = ds(i * 256, 256, 256)
            values[rows, :] = jnp.dot(xy[rows, :], rhs[h], preferred_element_type=F32)
            return carry

        lax.fori_loop(0, 4, predict, 0)

        def part(at, sub):
            return ds(((y + at) % 4) * 256 + sub * 128, 128, 128)

        up1 = send(values.at[part(2, 0)], am1.at[h, 0], y_next)
        down1 = send(values.at[part(2, 1)], am1.at[h, 1], y_prev)
        up2 = send(values.at[part(1, 1)], ar.at[h, 1, 0], y_next)
        down2 = send(values.at[part(3, 0)], ar.at[h, 0, 1], y_prev)
        yield 3.0
        up1.wait_recv()
        am3[h, 0] = values[part(1, 0), :] + am1[h, 0]
        up3 = send(am3.at[h, 0], ar.at[h, 0, 0], y_next)
        down1.wait_recv()
        am3[h, 1] = values[part(3, 1), :] + am1[h, 1]
        down3 = send(am3.at[h, 1], ar.at[h, 1, 1], y_prev)
        yield 5.7
        for copy in (up2, down2, up3, down3):
            copy.wait_recv()
        zs[h] = values[part(0, 1 - zl), :] + ar[h, 1 - zl, 0] + ar[h, 1 - zl, 1]
        pair = send(zs.at[h], zr.at[h], z_pair)
        mine = values[part(0, zl), :] + ar[h, zl, 0] + ar[h, zl, 1]
        top, bottom = obsv[0], obsv[1]
        low = lane_low((128, 128))
        if h == 0:
            mine -= jnp.where(low, top, swap_lanes(bottom))
        else:
            mine -= jnp.where(low, swap_lanes(top), bottom)
        zs2 = resp.at[h, 0]
        zs2[part(0, zl), :] = mine
        yield 8.5
        pair.wait_recv()
        zs2[part(0, zl), :] += zr[h]

        def share(at, sub, first, size, to):
            start = ((y + at) % 4) * 256 + sub * 128 + first
            rows = ds(start, size, 64)
            return send(zs2.at[rows], zs2.at[rows], to)

        up1 = share(0, zl, 0, 128, y_next)
        down1 = share(0, zl, 0, 128, y_prev)
        pair = share(0, zl, 0, 128, z_pair)
        yield 11.3
        up1.wait_recv()
        up2 = share(3, zl, 0, 64, y_next)
        down1.wait_recv()
        down2 = share(1, zl, 64, 64, y_prev)
        pair.wait_recv()
        up3 = share(0, 1 - zl, 0, 128, y_next)
        down3 = share(0, 1 - zl, 0, 128, y_prev)
        yield 14.0
        up3.wait_recv()
        up4 = share(3, 1 - zl, 0, 64, y_next)
        down3.wait_recv()
        down4 = share(1, 1 - zl, 64, 64, y_prev)
        yield 16.0
        for copy in (up2, down2, up4, down4):
            copy.wait_recv()

        half = zs2[...].astype(BF16)
        low = lane_low((64, 128))
        acc = []
        for i in range(2):
            acc.append(jnp.dot(xyt[pl.ds(i * 256, 256), :], half, preferred_element_type=F32))
        total = acc[0] + swap_lanes(acc[1])
        turned = swap_lanes(total)
        bsend[h] = jnp.where(low, total[128:192], turned[192:256])
        swap = send(bsend.at[h], brecv.at[h], sibling)
        mine = jnp.where(low, total[0:64], turned[64:128])
        copies = [send(zs2, resp.at[h, 1], sibling)]
        yield 18.5
        swap.wait_recv()
        k_index = lax.broadcasted_iota(jnp.int32, (64, 128), 0) + jnp.where(low, 0, 64)
        mine = jnp.where(k_index < rank[0, 0], mine + brecv[h], 0.0)
        bx[h, 0] = mine.astype(BF16).astype(F32)
        copies += [
            send(bx.at[h, 0], bx.at[h, 1], x_prev),
            send(bx.at[h, 0], bx.at[h, 2], x_far),
            send(bx.at[h, 0], bx.at[h, 3], x_next),
        ]
        yield 21.5
        for copy in copies[1:]:
            copy.wait_recv()
        for d in range(4):
            packed = bx[h, d]
            turned = swap_lanes(packed)
            bd[h, pl.ds(d * 256, 64), :] = jnp.where(low, packed, 0.0).astype(BF16)
            bd[h, pl.ds(d * 256 + 64, 64), :] = jnp.where(low, turned, 0.0).astype(BF16)
            bd[h, pl.ds(d * 256 + 128, 64), :] = jnp.where(low, 0.0, turned).astype(BF16)
            bd[h, pl.ds(d * 256 + 192, 64), :] = jnp.where(low, 0.0, packed).astype(BF16)

        part_grad = grad.at[h]

        def gradient(i, carry):
            rows = ds(i * 256, 256, 256)
            part_grad[rows, :] = jnp.dot(grcat[rows, :], bd[h], preferred_element_type=F32)
            return carry

        lax.fori_loop(0, 2, gradient, 0)

        def piece(at, sub):
            return ds(((zh + at) % 4) * 128 + sub * 64, 64, 64)

        up1 = send(part_grad.at[piece(2, 0)], cm1.at[h, 0], zh_next)
        down1 = send(part_grad.at[piece(2, 1)], cm1.at[h, 1], zh_prev)
        up2 = send(part_grad.at[piece(1, 1)], cr.at[h, 1, 0], zh_next)
        down2 = send(part_grad.at[piece(3, 0)], cr.at[h, 0, 1], zh_prev)
        yield 25.0
        up1.wait_recv()
        cm3[h, 0] = part_grad[piece(1, 0), :] + cm1[h, 0]
        up3 = send(cm3.at[h, 0], cr.at[h, 0, 0], zh_next)
        down1.wait_recv()
        cm3[h, 1] = part_grad[piece(3, 1), :] + cm1[h, 1]
        down3 = send(cm3.at[h, 1], cr.at[h, 1, 1], zh_prev)
        yield 28.0
        for copy in (up2, down2, up3, down3):
            copy.wait_recv()
        final = outp.at[h]
        for sub in range(2):
            total = part_grad[piece(0, sub), :] + cr[h, sub, 0] + cr[h, sub, 1]
            rows = ds(row * 128 + sub * 64, 64, 64)
            final[rows, :] = jnp.maximum(base[h, pl.ds(sub * 64, 64), :] - 0.5 * total, 0.0)

        def spread(x_at, zh_at, first, size, to):
            start = (((x + x_at) % 4) * 4 + (zh + zh_at) % 4) * 128 + first
            rows = ds(start, size, 64)
            return send(final.at[rows], final.at[rows], to)

        z_up1 = spread(0, 0, 0, 128, zh_next)
        z_down1 = spread(0, 0, 0, 128, zh_prev)
        x_up, x_down, last = {}, {}, []
        x_up[0] = spread(0, 0, 0, 128, x_next)
        x_down[0] = spread(0, 0, 0, 128, x_prev)

        def pass_on(at):
            x_up[at].wait_recv()
            last.append(spread(3, at, 0, 64, x_next))
            x_down[at].wait_recv()
            last.append(spread(1, at, 64, 64, x_prev))

        yield 32.5
        z_up1.wait_recv()
        z_up2 = spread(0, 3, 0, 64, zh_next)
        x_up[3] = spread(0, 3, 0, 128, x_next)
        x_down[3] = spread(0, 3, 0, 128, x_prev)
        z_down1.wait_recv()
        z_down2 = spread(0, 1, 64, 64, zh_prev)
        x_up[1] = spread(0, 1, 0, 128, x_next)
        x_down[1] = spread(0, 1, 0, 128, x_prev)
        pass_on(0)
        yield 36.0
        z_up2.wait_recv()
        z_down2.wait_recv()
        x_up[2] = spread(0, 2, 0, 128, x_next)
        x_down[2] = spread(0, 2, 0, 128, x_prev)
        pass_on(3)
        yield 37.5
        pass_on(1)
        yield 39.0
        pass_on(2)
        yield 41.0
        for copy in last:
            copy.wait_recv()
        copies[0].wait_recv()

    def side():
        yield 0.1

        def turn(i, carry):
            rows = ds(i * 128, 128, 128)
            for j in range(4):
                xyt[pl.ds(j * 128, 128), rows] = xy[rows, pl.ds(j * 128, 128)].T
            return carry

        lax.fori_loop(0, 8, turn, 0)
        yield 7.5
        load_nbr.wait()
        for copy in halo:
            copy.wait_recv()
        first = col * 2048 + row * 128 - HALO
        place = lax.broadcasted_iota(jnp.int32, (256, 128), 0) + first
        links = jnp.zeros((256, 128), F32)
        for index in range(8):
            links += (nbrv[pl.ds(index, 1), :] == place).astype(F32)
        links = links.astype(BF16)
        window = ext[ds(row * 128, 256, 128), :]
        high = window.astype(BF16)
        rest = (window - high.astype(F32)).astype(BF16)
        dims = (((0,), (0,)), ((), ()))
        near = lax.dot_general(links, high, dims, preferred_element_type=F32)
        near += lax.dot_general(links, rest, dims, preferred_element_type=F32)
        own = ext[ds(row * 128 + HALO, 128, 64), :]
        wide = own - 0.025 * (8.0 * own - near)
        left, right = wide[:, :128], wide[:, 128:]
        low = lane_low((128, 128))
        base[0] = jnp.where(low, left, swap_lanes(right))
        base[1] = jnp.where(low, swap_lanes(left), right)
        grcat[:, pl.ds(0, 256)] = grv[x_block(0), :]
        yield 20.9
        for d in range(1, 4):
            share_gr[d - 1].wait_recv()
            grcat[:, pl.ds(d * 256, 256)] = grrecv[d - 1].astype(BF16)

    tasks = [(0.0, 0, chain(0)), (0.05, 1, chain(1)), (0.06, 2, side())]
    shift = {0: 0.0, 1: 3.9, 2: 0.0}
    while tasks:
        tasks.sort(key=lambda task: task[:2])
        _, number, task = tasks.pop(0)
        at = next(task, None)
        if at is not None:
            tasks.append((at + shift[number], number, task))

    def join_res(i, carry):
        low = lane_low((128, 128))
        rows = ds(i * 128, 128, 128)
        for half in range(2):
            first, second = resp[0, half, rows, :], resp[1, half, rows, :]
            at = (k if half == 0 else 1 - k) * 2048 + i * 128
            resv[ds(at, 128, 128), :] = jnp.where(low, first, swap_lanes(second))
            resv[ds(at + 1024, 128, 128), :] = jnp.where(low, swap_lanes(first), second)
        return carry

    lax.fori_loop(0, 8, join_res, 0)
    store_res = local(resv, res)

    def join_out(i, carry):
        low = lane_low((128, 128))
        rows = ds(i * 128, 128, 128)
        first, second = outp[0, rows, :], outp[1, rows, :]
        outv[rows, pl.ds(0, 128)] = jnp.where(low, first, swap_lanes(second))
        outv[rows, pl.ds(128, 128)] = jnp.where(low, swap_lanes(first), second)
        return carry

    lax.fori_loop(0, 16, join_out, 0)
    store_out = local(outv, out)
    for copy in sends:
        copy.wait_send()
    store_res.wait()
    store_out.wait()


def body(observed, slip, green_left, green_right, block_ranks, neighbours):
    vmem, dma = pltpu.VMEM, pltpu.SemaphoreType.DMA
    hbm = pl.BlockSpec(memory_space=pl.ANY)
    return pl.pallas_call(
        kernel,
        name="step",
        out_shape=(
            jax.ShapeDtypeStruct((2048, 256), F32),
            jax.ShapeDtypeStruct((4096, 128), F32),
        ),
        in_specs=[hbm, hbm, hbm, hbm, pl.BlockSpec(memory_space=pltpu.SMEM), hbm],
        out_specs=(hbm, hbm),
        scratch_shapes=[
            vmem((2048 + 2 * HALO, 256), F32),
            vmem((4096, 128), BF16),
            vmem((2048, 256), BF16),
            vmem((2, 128, 128), F32),
            vmem((8, 128), jnp.int32),
            vmem((2048, 128), F32),
            vmem((2048, 128), F32),
            vmem((1024, 512), BF16),
            vmem((512, 1024), BF16),
            vmem((2048, 256), F32),
            vmem((3, 512, 256), F32),
            vmem((512, 1024), BF16),
            vmem((128, 128), F32),
            vmem((128, 128), F32),
            vmem((2, 512, 128), BF16),
            vmem((2, 1024, 128), F32),
            vmem((2, 2, 128, 128), F32),
            vmem((2, 2, 2, 128, 128), F32),
            vmem((2, 2, 128, 128), F32),
            vmem((2, 128, 128), F32),
            vmem((2, 128, 128), F32),
            vmem((2, 2, 1024, 128), F32),
            vmem((2, 64, 128), F32),
            vmem((2, 64, 128), F32),
            vmem((2, 4, 64, 128), F32),
            vmem((2, 1024, 128), BF16),
            vmem((2, 512, 128), F32),
            vmem((2, 2, 64, 128), F32),
            vmem((2, 2, 2, 64, 128), F32),
            vmem((2, 2, 64, 128), F32),
            vmem((2, 128, 128), F32),
            vmem((2, 2048, 128), F32),
            vmem((2048, 256), F32),
            vmem((4096, 128), F32),
            dma((N_SEM,)),
            dma((N_SEM,)),
            dma((32,)),
        ],
        compiler_params=pltpu.CompilerParams(
            collective_id=0, has_side_effects=True, vmem_limit_bytes=48 * 2**20
        ),
        cost_estimate=pl.CostEstimate(flops=10**9, bytes_accessed=12 * 2**20, transcendentals=0),
    )(observed, slip, green_left, green_right, block_ranks, neighbours.T)


def solution(mesh):
    return jax.shard_map(
        body,
        mesh=mesh,
        in_specs=(
            P("row", None),
            P("col", None),
            P("row", "col"),
            P("col", "row"),
            P("row", "col"),
            P("col", None),
        ),
        out_specs=(P("col", None), P("row", None)),
        check_vma=False,
    )
```

time: 362 us -> 92.4 us (0.26); the launches traced: 356 us -> 91.1 us
  waiting for transfers between devices: 234 us -> 0 us
  Pallas kernels: 0 us -> 82.8 us
  local copies, waits for them, and re-layouts: 78.6 us -> 6.94 us
  other arithmetic: 17.6 us -> 0 us
  between operations: 14.8 us -> 1.3 us
  matrix products: 7.77 us -> 0 us
    psum x2 -> x0, waiting for transfers between devices: 234 us -> none  [the longest x1 129 us: body(): residual = lax.psum(predicted, 'col') - observed]
    pallas_call x0 -> x1, Pallas kernels: none -> 82.8 us  [body(): pl.pallas_call(kernel, name='step', out_shape=(jax.ShapeDtypeStruct((2048...]
    gather x8 -> x0, local copies, waits for them, and re-layouts: 68.7 us -> none  [body(): smooth = smooth - jnp.take(extended, local_index[:, index], axis=0)]
    max x1 -> x0, other arithmetic: 10.3 us -> none  [body(): slip_next = jnp.maximum(slip - 0.5 * (gradient + 0.05 * smooth), 0.0)]
    dot_general x2 -> x0, matrix products: 7.77 us -> none  [the longest x1 3.98 us: body(): jnp.einsum('pak,kn->pan', right_view, back_half, preferred_element_type=j...]
    sub x2 -> x0, other arithmetic: 3.81 us -> none  [the longest x1 3.8 us: body(): residual = lax.psum(predicted, 'col') - observed]
  transfers between devices with their start and end apart: 4 -> 0, of which waited for: 3 -> 0; matrix products, arithmetic and copies ran while one was open for 24% -> 0% of each run, Pallas kernels for 0% -> 0%
where the time goes in v1:
time: 92.4 us; the launch traced here: 91.1 us
  Pallas kernels  82.8 us (90%)
  local copies, waits for them, and re-layouts  6.94 us (8%)
  between operations  1.3 us (1%)
    pallas_call x1, Pallas kernels, body(): pl.pallas_call(kernel, name='step', out_shape=(jax.ShapeDtypeStruct((2048...  82.8 us
    unnamed x10, local copies, waits for them, and re-layouts  6.94 us

profile of v1, /device:TPU:2, one launch (start us, length us, event | category | flops | bytes accessed | tf_op | source)
XLA Modules:
  0.0 91.1 jit_solution(3542491600005556052)
XLA Ops:
  1.3 0.0 copy-start
  1.3 1.2 %copy-done = bf16[4096,128]{1,0:T(8,128)(2,1)S(1)} copy-done((bf16[4096,128]{1,0:T(8,128)(2,1)S(1)}, bf16[4096,128]{1,0:T(8,128)(2,1)}, u32[]{:S(2)}) %copy-start) | copy-done | bytes 1048600
  2.5 0.0 copy-start.1
  2.5 1.2 %copy-done.1 = bf16[2048,256]{1,0:T(8,128)(2,1)S(1)} copy-done((bf16[2048,256]{1,0:T(8,128)(2,1)S(1)}, bf16[2048,256]{1,0:T(8,128)(2,1)}, u32[]{:S(2)}) %copy-start.1) | copy-done | bytes 1048600
  3.7 0.0 copy-start.2
  3.7 0.8 copy-done.2
  4.6 82.8 %step.1 = (f32[2048,256]{1,0:T(8,128)S(1)}, f32[4096,128]{1,0:T(8,128)}) custom-call(f32[4096,128]{1,0:T(8,128)} %obs.1, f32[2048,256]{1,0:T(8,128)} %slip.1, bf16[4096,128]{1,0:T(8,128)(2,1)S(1)} %copy-done, bf16[2048,256]{1,0:T(8,128)(2,1)S(1)} %copy-done.1, s32[1,1]{1,0:T(1,128)S(6)} %copy.10.rank, s32[8,2048]{1,0:T(8,128)S(1)} %bitcast.1), custom_call_target="tpu_custom_call" | custom-call | flops 1000000000 | bytes 12582912 | tf_op jit(solution)/shard_map/step/pallas_call | solution.py:429
  87.4 0.0 copy-start.3
  87.4 1.3 %copy.11 = f32[2048,256]{1,0:T(8,128)} copy(f32[2048,256]{1,0:T(8,128)S(1)} %get-tuple-element.4) | data formatting | bytes 4194304
  88.8 1.0 %copy-done.3 = f32[4096,128]{1,0:T(8,128)S(1)} copy-done((f32[4096,128]{1,0:T(8,128)S(1)}, f32[4096,128]{1,0:T(8,128)}, u32[]{:S(2)}) %copy-start.3) | copy-done | bytes 2097176
  89.8 1.3 %copy.12 = f32[4096,128]{1,0:T(8,128)} copy(f32[4096,128]{1,0:T(8,128)S(1)} %copy-done.3) | data formatting | bytes 4194304
Async XLA Ops:
  1.3 1.2 %copy-start = (bf16[4096,128]{1,0:T(8,128)(2,1)S(1)}, bf16[4096,128]{1,0:T(8,128)(2,1)}, u32[]{:S(2)}) copy-start(bf16[4096,128]{1,0:T(8,128)(2,1)} %gl.1) | copy-start | bytes 3145732
  2.5 1.2 %copy-start.1 = (bf16[2048,256]{1,0:T(8,128)(2,1)S(1)}, bf16[2048,256]{1,0:T(8,128)(2,1)}, u32[]{:S(2)}) copy-start(bf16[2048,256]{1,0:T(8,128)(2,1)} %gr.1) | copy-start | bytes 3145732
  3.7 0.8 copy-start.2
  87.4 2.3 %copy-start.3 = (f32[4096,128]{1,0:T(8,128)S(1)}, f32[4096,128]{1,0:T(8,128)}, u32[]{:S(2)}) copy-start(f32[4096,128]{1,0:T(8,128)} %get-tuple-element.5) | copy-start | bytes 6291460

commit v2 on v1

v2 whole, which is shorter than its diff:
```python
import jax
import jax.numpy as jnp
from jax import lax
from jax.experimental import pallas as pl
from jax.experimental.pallas import tpu as pltpu
from jax.sharding import PartitionSpec as P

MESH = pl.DeviceIdType.MESH
F32 = jnp.float32
BF16 = jnp.bfloat16
HALO = 64
N_SEM = 160


def lane_low(shape):
    return lax.broadcasted_iota(jnp.int32, shape, 1) < 64


def swap_lanes(value):
    return pltpu.roll(value, 64, 1)


def ds(start, size, unit):
    if isinstance(start, int):
        return pl.ds(start, size)
    return pl.ds(pl.multiple_of(start, unit), size)


def kernel(
    obs, slip, gl, gr, rank, nbr, out, res,
    ext, glv, grv, obsv, nbrv, glsend, glrecv, xy, xyt, grsend, grrecv, grcat,
    insend, inrecv, rhs, pred, azr, azs, ay, af, afs, resp, bsend, brecv, bx, bd, grad,
    cm1, cr, cm3, base, outp, send_sem, recv_sem, local_sem,
):
    row = lax.axis_index("row")
    col = lax.axis_index("col")
    x, zh = row // 4, row % 4
    zl, y, k = col // 8, (col // 2) % 4, col % 2

    def device(x, zh, zl, y, k):
        return (x * 4 + zh, (zl * 4 + y) * 2 + k)

    sibling = device(x, zh, zl, y, 1 - k)
    y_next = device(x, zh, zl, (y + 1) % 4, k)
    y_prev = device(x, zh, zl, (y + 3) % 4, k)
    y_far = device(x, zh, zl, (y + 2) % 4, k)
    z_pair = device(x, zh, 1 - zl, y, k)
    x_next = device((x + 1) % 4, zh, zl, y, k)
    x_prev = device((x + 3) % 4, zh, zl, y, k)
    x_far = device((x + 2) % 4, zh, zl, y, k)
    zh_next = device(x, (zh + 1) % 4, zl, y, k)
    zh_prev = device(x, (zh + 3) % 4, zl, y, k)
    col_next = (row, (col + 1) % 16)
    col_prev = (row, (col + 15) % 16)

    counts = [0, 0]
    sends = []

    def send(src, dst, to):
        index = counts[0]
        counts[0] += 1
        copy = pltpu.make_async_remote_copy(
            src_ref=src, dst_ref=dst, send_sem=send_sem.at[index], recv_sem=recv_sem.at[index],
            device_id=to, device_id_type=MESH,
        )
        copy.start()
        sends.append(copy)
        return copy

    def local(src, dst):
        index = counts[1]
        counts[1] += 1
        copy = pltpu.make_async_copy(src, dst, local_sem.at[index])
        copy.start()
        return copy

    partners = (
        sibling, col_next, col_prev, zh_next, zh_prev, x_next, x_prev, x_far, y_next, y_prev, y_far, z_pair,
    )

    load_gl = [
        local(gl.at[ds((1 - k) * 2048, 2048, 2048)], glv.at[pl.ds(2048, 2048)]),
    ]
    load_gr, load_slip = [], []
    for piece in range(4):
        rows = pl.ds(piece * 512, 512)
        load_gr.append(local(gr.at[rows], grv.at[rows]))
        load_slip.append(local(slip.at[rows], ext.at[pl.ds(HALO + piece * 512, 512)]))
    load_gl.append(local(gl.at[ds(k * 2048, 2048, 2048)], glv.at[pl.ds(0, 2048)]))
    shard = y * 256 + zl * 128
    load_obs = [
        local(obs.at[ds(k * 2048 + half * 1024 + shard, 128, 128)], obsv.at[half]) for half in range(2)
    ]
    load_nbr = local(nbr.at[:, ds(row * 128, 128, 128)], nbrv)

    barrier = pltpu.get_barrier_semaphore()
    for partner in partners:
        pl.semaphore_signal(barrier, inc=1, device_id=partner, device_id_type=MESH)

    keep = lax.broadcasted_iota(jnp.int32, (128, 128), 0) < rank[0, 0]
    keep_lane = lax.broadcasted_iota(jnp.int32, (256, 128), 1) < rank[0, 0]
    early = {}

    def x_block(at):
        return ds(((x + at) % 4) * 512, 512, 512)

    def start():
        load_gl[0].wait()

        def widen_left(i, carry):
            rows = ds(i * 256, 256, 256)
            left = glv[ds(2048 + i * 256, 256, 256), :].astype(F32)
            glsend[rows, :] = jnp.where(keep_lane, left, 0.0)
            return carry

        lax.fori_loop(0, 8, widen_left, 0)
        yield -9.0
        pl.semaphore_wait(barrier, len(partners))
        swap_gl = [
            send(glsend.at[pl.ds(i * 512, 512)], glrecv.at[pl.ds(i * 512, 512)], sibling) for i in range(4)
        ]
        yield -8.0
        inner = jnp.zeros((128, 128), F32)
        for piece in range(4):
            load_gr[piece].wait()
            load_slip[piece].wait()
            for rake in range(2):
                lanes = pl.ds(rake * 128, 128)
                inner += lax.dot_general(
                    grv[pl.ds(piece * 512, 512), lanes],
                    ext[pl.ds(HALO + piece * 512, 512), lanes].astype(BF16),
                    (((0,), (0,)), ((), ())),
                    preferred_element_type=F32,
                )
        inner = jnp.where(keep, inner, 0.0).astype(BF16).astype(F32)
        insend[...] = inner
        swap_inner = send(insend, inrecv, sibling)
        yield -7.0

        def widen_right(i, carry):
            rows = ds(i * 256, 256, 256)
            grsend[rows, :] = grv[rows, :].astype(F32)
            return carry

        lax.fori_loop(0, 8, widen_right, 0)
        early["gr"] = [
            send(grsend.at[x_block(3)], grrecv.at[0], x_prev),
            send(grsend.at[x_block(2)], grrecv.at[1], x_far),
            send(grsend.at[x_block(1)], grrecv.at[2], x_next),
        ]
        early["halo"] = [
            send(ext.at[pl.ds(2048, HALO)], ext.at[pl.ds(0, HALO)], col_next),
            send(ext.at[pl.ds(HALO, HALO)], ext.at[pl.ds(2048 + HALO, HALO)], col_prev),
        ]
        yield -6.0
        load_gl[1].wait()

        def own_left(i, carry):
            rows = ds(i * 256, 256, 256)
            for half in range(2):
                left = glv[ds(half * 1024 + i * 256, 256, 256), :].astype(F32)
                xy[rows, pl.ds(half * 256, 128)] = jnp.where(keep_lane, left, 0.0).astype(BF16)
            return carry

        lax.fori_loop(0, 4, own_left, 0)
        yield -5.0
        for copy in swap_gl:
            copy.wait_recv()

        def other_left(i, carry):
            rows = ds(i * 256, 256, 256)
            for half in range(2):
                xy[rows, pl.ds(half * 256 + 128, 128)] = glrecv[ds(half * 1024 + i * 256, 256, 256), :].astype(BF16)
            return carry

        lax.fori_loop(0, 4, other_left, 0)
        yield -4.0
        for copy in load_obs:
            copy.wait()
        swap_inner.wait_recv()
        low = lane_low((256, 128))
        both = jnp.concatenate([inner, inrecv[...]], axis=0)
        turned = swap_lanes(both)
        rhs[0, pl.ds(0, 256), :] = jnp.where(low, both, 0.0).astype(BF16)
        rhs[0, pl.ds(256, 256), :] = jnp.where(low, 0.0, turned).astype(BF16)
        rhs[1, pl.ds(0, 256), :] = jnp.where(low, turned, 0.0).astype(BF16)
        rhs[1, pl.ds(256, 256), :] = jnp.where(low, 0.0, both).astype(BF16)
        yield -3.0

    def chain(h):
        lag = 4.0 * h
        if h == 1:
            yield 2.0
        values = pred.at[h]

        def predict(i, carry):
            rows = ds(i * 256, 256, 256)
            values[rows, :] = jnp.dot(xy[rows, :], rhs[h], preferred_element_type=F32)
            return carry

        lax.fori_loop(0, 4, predict, 0)

        def part(at, sub):
            return ds(((y + at) % 4) * 256 + sub * 128, 128, 128)

        other = 1 - zl
        pair1 = send(values.at[part(2, other)], azr.at[h, 0], z_pair)
        up1 = send(values.at[part(1, other)], ay.at[h, 0], y_next)
        down1 = send(values.at[part(3, other)], ay.at[h, 1], y_prev)
        up2 = send(values.at[part(1, zl)], af.at[h, 0], y_next)
        down2 = send(values.at[part(3, zl)], af.at[h, 1], y_prev)
        yield 3.6 + lag
        up1.wait_recv()
        down1.wait_recv()
        azs[h] = values[part(0, other), :] + ay[h, 0] + ay[h, 1]
        pair2 = send(azs.at[h], azr.at[h, 1], z_pair)
        pair1.wait_recv()
        afs[h] = values[part(2, zl), :] + azr[h, 0]
        far = send(afs.at[h], af.at[h, 2], y_far)
        top, bottom = obsv[0], obsv[1]
        low = lane_low((128, 128))
        if h == 0:
            seen = jnp.where(low, top, swap_lanes(bottom))
        else:
            seen = jnp.where(low, swap_lanes(top), bottom)
        residual = resp.at[h, 0]
        residual[part(0, zl), :] = values[part(0, zl), :] - seen
        yield 8.0 + lag
        for copy in (up2, down2, pair2, far):
            copy.wait_recv()
        mine = residual.at[part(0, zl)]
        mine[...] = mine[...] + af[h, 0] + af[h, 1] + af[h, 2] + azr[h, 1]

        def share(at, sub, to):
            shard = residual.at[part(at, sub)]
            return send(shard, shard, to)

        pair1 = share(0, zl, z_pair)
        far = share(0, zl, y_far)
        up1 = share(0, zl, y_next)
        down1 = share(0, zl, y_prev)
        yield 11.8 + lag
        pair1.wait_recv()
        up2 = share(0, other, y_next)
        down2 = share(0, other, y_prev)
        yield 13.0 + lag
        far.wait_recv()
        pair2 = share(2, zl, z_pair)
        yield 16.8 + lag
        for copy in (up1, down1, up2, down2, pair2):
            copy.wait_recv()

        half = residual[...].astype(BF16)
        low = lane_low((64, 128))
        acc = []
        for i in range(2):
            acc.append(jnp.dot(xyt[pl.ds(i * 256, 256), :], half, preferred_element_type=F32))
        total = acc[0] + swap_lanes(acc[1])
        turned = swap_lanes(total)
        bsend[h] = jnp.where(low, total[128:192], turned[192:256])
        swap = send(bsend.at[h], brecv.at[h], sibling)
        mine = jnp.where(low, total[0:64], turned[64:128])
        yield 18.0 + lag
        swap.wait_recv()
        bx[h, 0] = (mine + brecv[h]).astype(BF16).astype(F32)
        shares = [
            send(bx.at[h, 0], bx.at[h, 2], x_far),
            send(bx.at[h, 0], bx.at[h, 1], x_prev),
            send(bx.at[h, 0], bx.at[h, 3], x_next),
        ]
        early[h] = send(residual, resp.at[h, 1], sibling)
        yield 22.0 + lag
        for copy in shares:
            copy.wait_recv()
        for d in range(4):
            packed = bx[h, d]
            turned = swap_lanes(packed)
            bd[h, pl.ds(d * 256, 64), :] = jnp.where(low, packed, 0.0).astype(BF16)
            bd[h, pl.ds(d * 256 + 64, 64), :] = jnp.where(low, turned, 0.0).astype(BF16)
            bd[h, pl.ds(d * 256 + 128, 64), :] = jnp.where(low, 0.0, turned).astype(BF16)
            bd[h, pl.ds(d * 256 + 192, 64), :] = jnp.where(low, 0.0, packed).astype(BF16)

        part_grad = grad.at[h]

        def gradient(i, carry):
            rows = ds(i * 256, 256, 256)
            part_grad[rows, :] = jnp.dot(grcat[rows, :], bd[h], preferred_element_type=F32)
            return carry

        lax.fori_loop(0, 2, gradient, 0)

        def piece(at, sub):
            return ds(((zh + at) % 4) * 128 + sub * 64, 64, 64)

        up1 = send(part_grad.at[piece(2, 0)], cm1.at[h, 0], zh_next)
        down1 = send(part_grad.at[piece(2, 1)], cm1.at[h, 1], zh_prev)
        up2 = send(part_grad.at[piece(1, 1)], cr.at[h, 1, 0], zh_next)
        down2 = send(part_grad.at[piece(3, 0)], cr.at[h, 0, 1], zh_prev)
        yield 27.0 + lag
        up1.wait_recv()
        cm3[h, 0] = part_grad[piece(1, 0), :] + cm1[h, 0]
        up3 = send(cm3.at[h, 0], cr.at[h, 0, 0], zh_next)
        down1.wait_recv()
        cm3[h, 1] = part_grad[piece(3, 1), :] + cm1[h, 1]
        down3 = send(cm3.at[h, 1], cr.at[h, 1, 1], zh_prev)
        yield 31.3 + lag
        for copy in (up2, down2, up3, down3):
            copy.wait_recv()
        final = outp.at[h]
        for sub in range(2):
            total = part_grad[piece(0, sub), :] + cr[h, sub, 0] + cr[h, sub, 1]
            rows = ds(row * 128 + sub * 64, 64, 64)
            final[rows, :] = jnp.maximum(base[h, pl.ds(sub * 64, 64), :] - 0.5 * total, 0.0)

        def spread(x_at, zh_at, first, size, to):
            start = (((x + x_at) % 4) * 4 + (zh + zh_at) % 4) * 128 + first
            rows = ds(start, size, 64)
            return send(final.at[rows], final.at[rows], to)

        z_up1 = spread(0, 0, 0, 128, zh_next)
        z_down1 = spread(0, 0, 0, 128, zh_prev)
        x_up, x_down, last = {}, {}, {}
        x_up[0] = spread(0, 0, 0, 128, x_next)
        x_down[0] = spread(0, 0, 0, 128, x_prev)

        def pass_on(at):
            x_up[at].wait_recv()
            copies = [spread(3, at, 0, 64, x_next)]
            x_down[at].wait_recv()
            copies.append(spread(1, at, 64, 64, x_prev))
            last[at] = copies
            if h == 1:
                join(3, at)
                join(1, at)

        def finish(at):
            for copy in last[at]:
                copy.wait_recv()
            if h == 1:
                join(2, at)

        yield 35.2 + lag
        if h == 1:
            join(0, 0)
        pass_on(0)
        yield 37.2 + lag
        z_up1.wait_recv()
        z_up2 = spread(0, 3, 0, 64, zh_next)
        x_up[3] = spread(0, 3, 0, 128, x_next)
        x_down[3] = spread(0, 3, 0, 128, x_prev)
        z_down1.wait_recv()
        z_down2 = spread(0, 1, 64, 64, zh_prev)
        x_up[1] = spread(0, 1, 0, 128, x_next)
        x_down[1] = spread(0, 1, 0, 128, x_prev)
        if h == 1:
            join(0, 3)
            join(0, 1)
        yield 41.3 + lag
        z_up2.wait_recv()
        z_down2.wait_recv()
        x_up[2] = spread(0, 2, 0, 128, x_next)
        x_down[2] = spread(0, 2, 0, 128, x_prev)
        if h == 1:
            x_last = spread(0, 2, 0, 128, x_far)
            join(0, 2)
        finish(0)
        yield 41.6 + lag
        pass_on(3)
        yield 41.7 + lag
        pass_on(1)
        yield 45.0 + lag
        if h == 0:
            pass_on(2)
        else:
            x_up[2].wait_recv()
            join(3, 2)
            x_down[2].wait_recv()
            join(1, 2)
        finish(3)
        finish(1)
        yield 47.0 + lag
        if h == 0:
            finish(2)
        else:
            x_last.wait_recv()
            join(2, 2)

    def join(x_at, zh_at):
        low = lane_low((128, 128))
        rows = ds((((x + x_at) % 4) * 4 + (zh + zh_at) % 4) * 128, 128, 128)
        first, second = outp[0, rows, :], outp[1, rows, :]
        out[rows, pl.ds(0, 128)] = jnp.where(low, first, swap_lanes(second))
        out[rows, pl.ds(128, 128)] = jnp.where(low, swap_lanes(first), second)

    def join_res(half):
        def join_rows(i, carry):
            low = lane_low((128, 128))
            rows = ds(i * 128, 128, 128)
            first, second = resp[0, half, rows, :], resp[1, half, rows, :]
            at = (k if half == 0 else 1 - k) * 2048 + i * 128
            res[ds(at, 128, 128), :] = jnp.where(low, first, swap_lanes(second))
            res[ds(at + 1024, 128, 128), :] = jnp.where(low, swap_lanes(first), second)
            return carry

        lax.fori_loop(0, 8, join_rows, 0)

    def side():
        yield 0.1

        def turn(i, carry):
            rows = ds(i * 128, 128, 128)
            for j in range(4):
                xyt[pl.ds(j * 128, 128), rows] = xy[rows, pl.ds(j * 128, 128)].T
            return carry

        lax.fori_loop(0, 8, turn, 0)
        yield 8.2
        load_nbr.wait()
        for copy in early["halo"]:
            copy.wait_recv()
        first = col * 2048 + row * 128 - HALO
        place = lax.broadcasted_iota(jnp.int32, (256, 128), 0) + first
        links = jnp.zeros((256, 128), F32)
        for index in range(8):
            links += (nbrv[pl.ds(index, 1), :] == place).astype(F32)
        links = links.astype(BF16)
        window = ext[ds(row * 128, 256, 128), :]
        high = window.astype(BF16)
        rest = (window - high.astype(F32)).astype(BF16)
        dims = (((0,), (0,)), ((), ()))
        near = lax.dot_general(links, high, dims, preferred_element_type=F32)
        near += lax.dot_general(links, rest, dims, preferred_element_type=F32)
        own = ext[ds(row * 128 + HALO, 128, 64), :]
        wide = own - 0.025 * (8.0 * own - near)
        left, right = wide[:, :128], wide[:, 128:]
        low = lane_low((128, 128))
        base[0] = jnp.where(low, left, swap_lanes(right))
        base[1] = jnp.where(low, swap_lanes(left), right)
        grcat[:, pl.ds(0, 256)] = grv[x_block(0), :]
        yield 18.2
        for d in range(1, 4):
            early["gr"][d - 1].wait_recv()
            grcat[:, pl.ds(d * 256, 256)] = grrecv[d - 1].astype(BF16)

        yield 27.6
        join_res(0)
        yield 35.5
        for h in range(2):
            early[h].wait_recv()
        join_res(1)

    tasks = [(-10.0, 3, start())]
    while tasks:
        tasks.sort(key=lambda task: task[:2])
        _, number, task = tasks.pop(0)
        at = next(task, None)
        if at is not None:
            tasks.append((at, number, task))
        elif number == 3:
            tasks = [(0.0, 0, chain(0)), (0.05, 1, chain(1)), (0.06, 2, side())]
    for copy in sends:
        copy.wait_send()


def store(out_in, res_in, out, res, sem):
    copies = [
        pltpu.make_async_copy(out_in, out, sem.at[0]),
        pltpu.make_async_copy(res_in, res, sem.at[1]),
    ]
    for copy in copies:
        copy.start()
    for copy in copies:
        copy.wait()


def body(observed, slip, green_left, green_right, block_ranks, neighbours):
    vmem, dma = pltpu.VMEM, pltpu.SemaphoreType.DMA
    hbm = pl.BlockSpec(memory_space=pltpu.HBM)
    whole = pl.BlockSpec(memory_space=pltpu.VMEM)
    shapes = (
        jax.ShapeDtypeStruct((2048, 256), F32),
        jax.ShapeDtypeStruct((4096, 128), F32),
    )
    joined = pl.pallas_call(
        kernel,
        name="step",
        out_shape=tuple(vmem(shape.shape, F32) for shape in shapes),
        in_specs=[hbm, hbm, hbm, hbm, pl.BlockSpec(memory_space=pltpu.SMEM), hbm],
        out_specs=(whole, whole),
        scratch_shapes=[
            vmem((2048 + 2 * HALO, 256), F32),
            vmem((4096, 128), BF16),
            vmem((2048, 256), BF16),
            vmem((2, 128, 128), F32),
            vmem((8, 128), jnp.int32),
            vmem((2048, 128), F32),
            vmem((2048, 128), F32),
            vmem((1024, 512), BF16),
            vmem((512, 1024), BF16),
            vmem((2048, 256), F32),
            vmem((3, 512, 256), F32),
            vmem((512, 1024), BF16),
            vmem((128, 128), F32),
            vmem((128, 128), F32),
            vmem((2, 512, 128), BF16),
            vmem((2, 1024, 128), F32),
            vmem((2, 2, 128, 128), F32),
            vmem((2, 128, 128), F32),
            vmem((2, 2, 128, 128), F32),
            vmem((2, 3, 128, 128), F32),
            vmem((2, 128, 128), F32),
            vmem((2, 2, 1024, 128), F32),
            vmem((2, 64, 128), F32),
            vmem((2, 64, 128), F32),
            vmem((2, 4, 64, 128), F32),
            vmem((2, 1024, 128), BF16),
            vmem((2, 512, 128), F32),
            vmem((2, 2, 64, 128), F32),
            vmem((2, 2, 2, 64, 128), F32),
            vmem((2, 2, 64, 128), F32),
            vmem((2, 128, 128), F32),
            vmem((2, 2048, 128), F32),
            dma((N_SEM,)),
            dma((N_SEM,)),
            dma((32,)),
        ],
        compiler_params=pltpu.CompilerParams(
            collective_id=0, has_side_effects=True, vmem_limit_bytes=40 * 2**20
        ),
        cost_estimate=pl.CostEstimate(flops=10**9, bytes_accessed=12 * 2**20, transcendentals=0),
    )(*(pltpu.with_memory_space_constraint(value, pltpu.HBM) for value in (observed, slip, green_left, green_right)), block_ranks, pltpu.with_memory_space_constraint(neighbours.T, pltpu.HBM))
    return pl.pallas_call(
        store,
        name="store",
        out_shape=shapes,
        in_specs=[whole, whole],
        out_specs=(hbm, hbm),
        scratch_shapes=[dma((2,))],
    )(*joined)


def solution(mesh):
    return jax.shard_map(
        body,
        mesh=mesh,
        in_specs=(
            P("row", None),
            P("col", None),
            P("row", "col"),
            P("col", "row"),
            P("row", "col"),
            P("col", None),
        ),
        out_specs=(P("col", None), P("row", None)),
        check_vma=False,
    )
```

time: 92.4 us -> 83.6 us (0.905); the launches traced: 91.1 us -> 83.6 us
  local copies, waits for them, and re-layouts: 6.94 us -> 2.64 us
  Pallas kernels: 82.8 us -> 79.6 us
    unnamed x10 -> x4, local copies, waits for them, and re-layouts: 6.94 us -> 2.64 us
    pallas_call x1 -> x2, Pallas kernels: 82.8 us -> 79.6 us  [the longest x1 75.4 us: body(): pl.pallas_call(kernel, name='step', out_shape=tuple((vmem(shape.shape, F3...]
where the time goes in v2:
time: 83.6 us
  Pallas kernels  79.6 us (95%)
  local copies, waits for them, and re-layouts  2.64 us (3%)
  between operations  1.29 us (2%)
    pallas_call x1, Pallas kernels, body(): pl.pallas_call(kernel, name='step', out_shape=tuple((vmem(shape.shape, F3...  75.4 us
    pallas_call x1, Pallas kernels, body(): pl.pallas_call(store, name='store', out_shape=shapes, in_specs=[whole, wh...  4.25 us
    unnamed x4, local copies, waits for them, and re-layouts  2.64 us

profile of v2, /device:TPU:2, one launch (start us, length us, event | category | flops | bytes accessed | tf_op | source)
XLA Modules:
  0.0 83.6 jit_solution(15735842146322711944)
XLA Ops:
  1.3 75.4 %step.1 = (f32[2048,256]{1,0:T(8,128)S(1)}, f32[4096,128]{1,0:T(8,128)S(1)}) custom-call(f32[4096,128]{1,0:T(8,128)} %obs.1, f32[2048,256]{1,0:T(8,128)} %slip.1, bf16[4096,128]{1,0:T(8,128)(2,1)} %gl.1, bf16[2048,256]{1,0:T(8,128)(2,1)} %gr.1, s32[1,1]{1,0:T(1,128)S(6)} %copy.8.rank, s32[8,2048]{1,0:T(8,128)} %bitcast.1), custom_call_target="tpu_custom_call" | custom-call | flops 1000000000 | bytes 12582912 | tf_op jit(solution)/shard_map/step/pallas_call | solution.py:484
  76.7 0.0 copy-start
  76.7 1.3 %copy-done = f32[2048,256]{1,0:T(8,128)} copy-done((f32[2048,256]{1,0:T(8,128)}, f32[2048,256]{1,0:T(8,128)S(1)}, u32[]{:S(2)}) %copy-start) | copy-done | bytes 2097176
  78.0 0.0 copy-start.1
  78.0 1.3 %copy-done.1 = f32[4096,128]{1,0:T(8,128)} copy-done((f32[4096,128]{1,0:T(8,128)}, f32[4096,128]{1,0:T(8,128)S(1)}, u32[]{:S(2)}) %copy-start.1) | copy-done | bytes 2097176
  79.3 4.2 %store.1 = (f32[2048,256]{1,0:T(8,128)}, f32[4096,128]{1,0:T(8,128)}) custom-call(f32[2048,256]{1,0:T(8,128)} %copy-done, f32[4096,128]{1,0:T(8,128)} %copy-done.1), custom_call_target="tpu_custom_call" | custom-call | tf_op jit(solution)/shard_map/store/pallas_call | solution.py:532
Async XLA Ops:
  76.7 1.3 %copy-start = (f32[2048,256]{1,0:T(8,128)}, f32[2048,256]{1,0:T(8,128)S(1)}, u32[]{:S(2)}) copy-start(f32[2048,256]{1,0:T(8,128)S(1)} %get-tuple-element.4.out_in) | copy-start | bytes 6291460
  78.0 1.3 %copy-start.1 = (f32[4096,128]{1,0:T(8,128)}, f32[4096,128]{1,0:T(8,128)S(1)}, u32[]{:S(2)}) copy-start(f32[4096,128]{1,0:T(8,128)S(1)} %get-tuple-element.5.res_in) | copy-start | bytes 6291460

commit v3 on v2

v3 whole, which is shorter than its diff:
```python
import jax
import jax.numpy as jnp
from jax import lax
from jax.experimental import pallas as pl
from jax.experimental.pallas import tpu as pltpu
from jax.sharding import PartitionSpec as P

MESH = pl.DeviceIdType.MESH
F32 = jnp.float32
BF16 = jnp.bfloat16
HALO = 64
N_SEM = 240
LAG_FORWARD, LAG_BACK = 3.5, 5.0
FAR_OVER_Z = ((0, 0), (0, 1), (1, 0), (1, 1))


def lane_low(shape):
    return lax.broadcasted_iota(jnp.int32, shape, 1) < 64


def swap_lanes(value):
    return pltpu.roll(value, 64, 1)


def ds(start, size, unit):
    if isinstance(start, int):
        return pl.ds(start, size)
    return pl.ds(pl.multiple_of(start, unit), size)


def kernel(
    obs, slip, gl, gr, rank, nbr, out, res,
    ext, glv, grv, obsv, nbrv, glsend, glrecv, xy, grsend, grrecv, grcat,
    rhs, pred, psend, precv, azr, azs, ay, af, afs, resp, bsend, brecv, bx, bd, grad,
    cm1, cr, cm3, base, outp, send_sem, recv_sem, local_sem,
):
    row = lax.axis_index("row")
    col = lax.axis_index("col")
    x, zh = row // 4, row % 4
    zl, y, k = col // 8, (col // 2) % 4, col % 2

    def device(x, zh, zl, y, k):
        return (x * 4 + zh, (zl * 4 + y) * 2 + k)

    sibling = device(x, zh, zl, y, 1 - k)
    y_next = device(x, zh, zl, (y + 1) % 4, k)
    y_prev = device(x, zh, zl, (y + 3) % 4, k)
    y_far = device(x, zh, zl, (y + 2) % 4, k)
    z_pair = device(x, zh, 1 - zl, y, k)
    x_next = device((x + 1) % 4, zh, zl, y, k)
    x_prev = device((x + 3) % 4, zh, zl, y, k)
    x_far = device((x + 2) % 4, zh, zl, y, k)
    zh_next = device(x, (zh + 1) % 4, zl, y, k)
    zh_prev = device(x, (zh + 3) % 4, zl, y, k)
    col_next = (row, (col + 1) % 16)
    col_prev = (row, (col + 15) % 16)

    counts = [0, 0]
    sends = []

    def send(src, dst, to):
        index = counts[0]
        counts[0] += 1
        copy = pltpu.make_async_remote_copy(
            src_ref=src, dst_ref=dst, send_sem=send_sem.at[index], recv_sem=recv_sem.at[index],
            device_id=to, device_id_type=MESH,
        )
        copy.start()
        sends.append(copy)
        return copy

    def local(src, dst):
        index = counts[1]
        counts[1] += 1
        copy = pltpu.make_async_copy(src, dst, local_sem.at[index])
        copy.start()
        return copy

    partners = (
        sibling, col_next, col_prev, zh_next, zh_prev, x_next, x_prev, x_far, y_next, y_prev, y_far, z_pair,
    )

    load_gr, load_slip = [], []
    for piece in range(4):
        rows = pl.ds(piece * 512, 512)
        load_gr.append(local(gr.at[rows], grv.at[rows]))
        load_slip.append(local(slip.at[rows], ext.at[pl.ds(HALO + piece * 512, 512)]))
    load_gl = [
        local(gl.at[ds((1 - k) * 2048, 2048, 2048)], glv.at[pl.ds(2048, 2048)]),
        local(gl.at[ds(k * 2048, 2048, 2048)], glv.at[pl.ds(0, 2048)]),
    ]
    shard = y * 128 + zl * 64
    load_obs = [
        local(obs.at[ds(k * 2048 + half * 1024 + piece * 512 + shard, 64, 64)], obsv.at[half, piece])
        for half in range(2)
        for piece in range(2)
    ]
    load_nbr = local(nbr.at[:, ds(row * 128, 128, 128)], nbrv)

    barrier = pltpu.get_barrier_semaphore()
    for partner in partners:
        pl.semaphore_signal(barrier, inc=1, device_id=partner, device_id_type=MESH)

    keep = lax.broadcasted_iota(jnp.int32, (128, 128), 0) < rank[0, 0]
    keep_lane = lax.broadcasted_iota(jnp.int32, (256, 128), 1) < rank[0, 0]
    early = {}

    def x_block(at):
        return ds(((x + at) % 4) * 512, 512, 512)

    def product(half, h, s):
        first = half * 2048 + s * 512
        pair = jnp.concatenate([glv[pl.ds(first, 512), :], glv[pl.ds(first + 1024, 512), :]], axis=1)
        return jnp.dot(pair, rhs[h], preferred_element_type=F32)

    def start():
        inner = jnp.zeros((128, 128), F32)
        for piece in range(4):
            load_gr[piece].wait()
            load_slip[piece].wait()
            for rake in range(2):
                lanes = pl.ds(rake * 128, 128)
                inner += lax.dot_general(
                    grv[pl.ds(piece * 512, 512), lanes],
                    ext[pl.ds(HALO + piece * 512, 512), lanes].astype(BF16),
                    (((0,), (0,)), ((), ())),
                    preferred_element_type=F32,
                )
        inner = jnp.where(keep, inner, 0.0).astype(BF16).astype(F32)
        low = lane_low((128, 128))
        turned = swap_lanes(inner)
        rhs[0, pl.ds(0, 128), :] = jnp.where(low, inner, 0.0).astype(BF16)
        rhs[0, pl.ds(128, 128), :] = jnp.where(low, 0.0, turned).astype(BF16)
        rhs[1, pl.ds(0, 128), :] = jnp.where(low, turned, 0.0).astype(BF16)
        rhs[1, pl.ds(128, 128), :] = jnp.where(low, 0.0, inner).astype(BF16)
        load_gl[0].wait()
        for h in range(2):
            for s in range(2):
                psend[h, s] = product(1, h, s)
        def widen_right(i, carry):
            rows = ds(i * 256, 256, 256)
            grsend[rows, :] = grv[rows, :].astype(F32)
            return carry

        lax.fori_loop(0, 8, widen_right, 0)
        yield -9.0
        pl.semaphore_wait(barrier, len(partners))
        for h in range(2):
            for s in range(2):
                early["pred", h, s] = [
                    send(psend.at[h, s, pl.ds(i * 128, 128)], precv.at[h, s, pl.ds(i * 128, 128)], sibling)
                    for i in range(4)
                ]
        early["gr"] = [
            send(grsend.at[x_block(3)], grrecv.at[0], x_prev),
            send(grsend.at[x_block(2)], grrecv.at[1], x_far),
            send(grsend.at[x_block(1)], grrecv.at[2], x_next),
        ]
        yield -8.0
        load_gl[1].wait()
        for h in range(2):
            for s in range(2):
                pred[h, s] = product(0, h, s)
        yield -7.0
        for copy in load_obs:
            copy.wait()

    def prepare():
        yield 1.0

        def widen_left(i, carry):
            rows = ds(i * 256, 256, 256)
            left = glv[ds(2048 + i * 256, 256, 256), :].astype(F32)
            glsend[rows, :] = jnp.where(keep_lane, left, 0.0)
            return carry

        lax.fori_loop(0, 8, widen_left, 0)
        early["gl"] = [
            send(glsend.at[pl.ds(i * 512, 512)], glrecv.at[pl.ds(i * 512, 512)], sibling) for i in range(4)
        ]
        early["halo"] = [
            send(ext.at[pl.ds(2048, HALO)], ext.at[pl.ds(0, HALO)], col_next),
            send(ext.at[pl.ds(HALO, HALO)], ext.at[pl.ds(2048 + HALO, HALO)], col_prev),
        ]
        yield 4.5

        def own_left(i, carry):
            rows = ds(i * 256, 256, 256)
            for half in range(2):
                left = glv[ds(half * 1024 + i * 256, 256, 256), :].astype(F32)
                xy[rows, pl.ds(half * 256, 128)] = jnp.where(keep_lane, left, 0.0).astype(BF16)
            return carry

        lax.fori_loop(0, 4, own_left, 0)
        yield 9.0
        for copy in early["gl"]:
            copy.wait_recv()

        def other_left(i, carry):
            rows = ds(i * 256, 256, 256)
            for half in range(2):
                xy[rows, pl.ds(half * 256 + 128, 128)] = glrecv[ds(half * 1024 + i * 256, 256, 256), :].astype(BF16)
            return carry

        lax.fori_loop(0, 4, other_left, 0)

    def forward(h, s):
        lag = LAG_FORWARD * h + 0.8 * s
        if h == 1:
            yield 2.0 + 0.1 * s
        values = pred.at[h, s]
        for copy in early["pred", h, s]:
            copy.wait_recv()
        values[...] += precv[h, s]

        def part(at, sub):
            return ds(((y + at) % 4) * 128 + sub * 64, 64, 64)

        other = 1 - zl
        pair1 = send(values.at[part(2, other)], azr.at[h, s, 0], z_pair)
        up1 = send(values.at[part(1, other)], ay.at[h, s, 0], y_next)
        down1 = send(values.at[part(3, other)], ay.at[h, s, 1], y_prev)
        up2 = send(values.at[part(1, zl)], af.at[h, s, 0], y_next)
        down2 = send(values.at[part(3, zl)], af.at[h, s, 1], y_prev)
        yield 3.0 + lag
        up1.wait_recv()
        down1.wait_recv()
        azs[h, s] = values[part(0, other), :] + ay[h, s, 0] + ay[h, s, 1]
        pair2 = send(azs.at[h, s], azr.at[h, s, 1], z_pair)
        pair1.wait_recv()
        afs[h, s] = values[part(2, zl), :] + azr[h, s, 0]
        far = send(afs.at[h, s], af.at[h, s, 2], y_far)
        top, bottom = obsv[0, s], obsv[1, s]
        low = lane_low((64, 128))
        if h == 0:
            seen = jnp.where(low, top, swap_lanes(bottom))
        else:
            seen = jnp.where(low, swap_lanes(top), bottom)
        residual = resp.at[h, 0, pl.ds(s * 512, 512)]
        mine = residual.at[part(0, zl)]
        mine[...] = values[part(0, zl), :] - seen
        yield 6.8 + lag
        for copy in (up2, down2, pair2, far):
            copy.wait_recv()
        mine[...] = mine[...] + af[h, s, 0] + af[h, s, 1] + af[h, s, 2] + azr[h, s, 1]

        def share(at, sub, to):
            shard = residual.at[part(at, sub)]
            return send(shard, shard, to)

        pair1 = share(0, zl, z_pair)
        far = share(0, zl, y_far)
        up1 = share(0, zl, y_next)
        down1 = share(0, zl, y_prev)
        yield 9.9 + lag
        pair1.wait_recv()
        up2 = share(0, other, y_next)
        down2 = share(0, other, y_prev)
        yield 10.4 + lag
        far.wait_recv()
        pair2 = share(2, zl, z_pair)
        yield 13.6 + lag
        for copy in (up1, down1, up2, down2, pair2):
            copy.wait_recv()

    def backward(h):
        lag = LAG_BACK * h
        yield 14.5 + lag
        residual = resp.at[h, 0]
        low = lane_low((64, 128))
        acc = lax.dot_general(
            xy[...], residual[...].astype(BF16), (((0,), (0,)), ((), ())), preferred_element_type=F32
        )
        total = acc[:256] + swap_lanes(acc[256:])
        turned = swap_lanes(total)
        bsend[h] = jnp.where(low, total[128:192], turned[192:256])
        swap = send(bsend.at[h], brecv.at[h], sibling)
        mine = jnp.where(low, total[0:64], turned[64:128])
        yield 16.2 + lag
        swap.wait_recv()
        bx[h, 0] = (mine + brecv[h]).astype(BF16).astype(F32)
        shares = [
            send(bx.at[h, 0], bx.at[h, 2], x_far),
            send(bx.at[h, 0], bx.at[h, 1], x_prev),
            send(bx.at[h, 0], bx.at[h, 3], x_next),
        ]
        early[h] = send(residual, resp.at[h, 1], sibling)
        yield 19.6 + lag
        for copy in shares:
            copy.wait_recv()
        for d in range(4):
            packed = bx[h, d]
            turned = swap_lanes(packed)
            bd[h, pl.ds(d * 256, 64), :] = jnp.where(low, packed, 0.0).astype(BF16)
            bd[h, pl.ds(d * 256 + 64, 64), :] = jnp.where(low, turned, 0.0).astype(BF16)
            bd[h, pl.ds(d * 256 + 128, 64), :] = jnp.where(low, 0.0, turned).astype(BF16)
            bd[h, pl.ds(d * 256 + 192, 64), :] = jnp.where(low, 0.0, packed).astype(BF16)

    def update(h, s):
        lag = LAG_BACK * h + 0.8 * s
        yield 19.7 + LAG_BACK * h + 0.01 * s
        part_grad = grad.at[h, s]
        part_grad[...] = jnp.dot(grcat[pl.ds(s * 256, 256), :], bd[h], preferred_element_type=F32)

        def piece(at, sub):
            return ds(((zh + at) % 4) * 64 + sub * 32, 32, 32)

        up1 = send(part_grad.at[piece(2, 0)], cm1.at[h, s, 0], zh_next)
        down1 = send(part_grad.at[piece(2, 1)], cm1.at[h, s, 1], zh_prev)
        up2 = send(part_grad.at[piece(1, 1)], cr.at[h, s, 1, 0], zh_next)
        down2 = send(part_grad.at[piece(3, 0)], cr.at[h, s, 0, 1], zh_prev)
        yield 23.8 + lag
        up1.wait_recv()
        cm3[h, s, 0] = part_grad[piece(1, 0), :] + cm1[h, s, 0]
        up3 = send(cm3.at[h, s, 0], cr.at[h, s, 0, 0], zh_next)
        down1.wait_recv()
        cm3[h, s, 1] = part_grad[piece(3, 1), :] + cm1[h, s, 1]
        down3 = send(cm3.at[h, s, 1], cr.at[h, s, 1, 1], zh_prev)
        yield 27.6 + lag
        for copy in (up2, down2, up3, down3):
            copy.wait_recv()
        final = outp.at[h]
        for sub in range(2):
            total = part_grad[piece(0, sub), :] + cr[h, s, sub, 0] + cr[h, s, sub, 1]
            rows = ds(row * 128 + s * 64 + sub * 32, 32, 32)
            final[rows, :] = jnp.maximum(base[h, pl.ds(s * 64 + sub * 32, 32), :] - 0.5 * total, 0.0)

        def spread(x_at, zh_at, first, size, to):
            start = (((x + x_at) % 4) * 4 + (zh + zh_at) % 4) * 128 + s * 64 + first
            rows = ds(start, size, 32)
            return send(final.at[rows], final.at[rows], to)

        def merge(x_at, zh_at):
            if h == 1:
                join(x_at, zh_at, s)

        far_over_z = (h, s) in FAR_OVER_Z
        z_up1 = spread(0, 0, 0, 64, zh_next)
        z_down1 = spread(0, 0, 0, 64, zh_prev)
        x_up, x_down, last = {}, {}, {}
        x_up[0] = spread(0, 0, 0, 64, x_next)
        x_down[0] = spread(0, 0, 0, 64, x_prev)
        if far_over_z:
            far = spread(0, 0, 0, 64, x_far)

        def send_x(at):
            x_up[at] = spread(0, at, 0, 64, x_next)
            x_down[at] = spread(0, at, 0, 64, x_prev)

        def pass_on(at):
            x_up[at].wait_recv()
            if not far_over_z:
                last[at] = [spread(3, at, 0, 32, x_next)]
            x_down[at].wait_recv()
            if not far_over_z:
                last[at].append(spread(1, at, 32, 32, x_prev))
            merge(3, at)
            merge(1, at)

        def finish(at):
            for copy in last[at]:
                copy.wait_recv()
            merge(2, at)

        yield 30.7 + lag
        merge(0, 0)
        pass_on(0)
        yield 32.2 + lag
        z_up1.wait_recv()
        z_up2 = spread(0, 3, 0, 32, zh_next)
        z_down1.wait_recv()
        z_down2 = spread(0, 1, 32, 32, zh_prev)
        send_x(3)
        send_x(1)
        merge(0, 3)
        merge(0, 1)
        if far_over_z:
            yield 32.3 + lag
            far.wait_recv()
            z_up3 = spread(2, 0, 0, 64, zh_next)
            z_down3 = spread(2, 0, 0, 64, zh_prev)
            merge(2, 0)
        yield 36.0 + lag
        z_up2.wait_recv()
        z_down2.wait_recv()
        send_x(2)
        merge(0, 2)
        direct = h == 1 and s == 1 and not far_over_z
        if direct:
            last[2] = [spread(0, 2, 0, 64, x_far)]
        if not far_over_z:
            finish(0)
        yield 36.1 + lag
        pass_on(3)
        yield 36.2 + lag
        pass_on(1)
        if far_over_z:
            yield 37.0 + lag
            z_up3.wait_recv()
            last[2] = [spread(2, 3, 0, 32, zh_next)]
            z_down3.wait_recv()
            last[2].append(spread(2, 1, 32, 32, zh_prev))
            merge(2, 3)
            merge(2, 1)
        yield 39.5 + lag
        if direct:
            x_up[2].wait_recv()
            merge(3, 2)
            x_down[2].wait_recv()
            merge(1, 2)
        else:
            pass_on(2)
        if not far_over_z:
            finish(3)
            finish(1)
        yield 41.5 + lag
        finish(2)

    def join(x_at, zh_at, s):
        low = lane_low((64, 128))
        rows = ds((((x + x_at) % 4) * 4 + (zh + zh_at) % 4) * 128 + s * 64, 64, 64)
        first, second = outp[0, rows, :], outp[1, rows, :]
        out[rows, pl.ds(0, 128)] = jnp.where(low, first, swap_lanes(second))
        out[rows, pl.ds(128, 128)] = jnp.where(low, swap_lanes(first), second)

    def join_res(half):
        def join_rows(i, carry):
            low = lane_low((128, 128))
            rows = ds(i * 128, 128, 128)
            first, second = resp[0, half, rows, :], resp[1, half, rows, :]
            at = (k if half == 0 else 1 - k) * 2048 + i * 128
            res[ds(at, 128, 128), :] = jnp.where(low, first, swap_lanes(second))
            res[ds(at + 1024, 128, 128), :] = jnp.where(low, swap_lanes(first), second)
            return carry

        lax.fori_loop(0, 8, join_rows, 0)

    def side():
        yield 7.0
        load_nbr.wait()
        for copy in early["halo"]:
            copy.wait_recv()
        first = col * 2048 + row * 128 - HALO
        place = lax.broadcasted_iota(jnp.int32, (256, 128), 0) + first
        links = jnp.zeros((256, 128), F32)
        for index in range(8):
            links += (nbrv[pl.ds(index, 1), :] == place).astype(F32)
        links = links.astype(BF16)
        window = ext[ds(row * 128, 256, 128), :]
        high = window.astype(BF16)
        rest = (window - high.astype(F32)).astype(BF16)
        dims = (((0,), (0,)), ((), ()))
        near = lax.dot_general(links, high, dims, preferred_element_type=F32)
        near += lax.dot_general(links, rest, dims, preferred_element_type=F32)
        own = ext[ds(row * 128 + HALO, 128, 64), :]
        wide = own - 0.025 * (8.0 * own - near)
        left, right = wide[:, :128], wide[:, 128:]
        low = lane_low((128, 128))
        base[0] = jnp.where(low, left, swap_lanes(right))
        base[1] = jnp.where(low, swap_lanes(left), right)
        for shard in range(4):
            for s in range(2):
                rows = ds((x * 4 + shard) * 128 + s * 64, 64, 64)
                grcat[pl.ds(s * 256 + shard * 64, 64), pl.ds(0, 256)] = grv[rows, :]
        yield 16.4
        for d in range(1, 4):
            early["gr"][d - 1].wait_recv()
            for shard in range(4):
                for s in range(2):
                    rows = pl.ds(shard * 128 + s * 64, 64)
                    grcat[pl.ds(s * 256 + shard * 64, 64), pl.ds(d * 256, 256)] = grrecv[d - 1, rows, :].astype(BF16)
        yield 24.8
        join_res(0)
        yield 30.0
        for h in range(2):
            early[h].wait_recv()
        join_res(1)

    tasks = [(-10.0, 99, start())]
    while tasks:
        tasks.sort(key=lambda task: task[:2])
        _, number, task = tasks.pop(0)
        at = next(task, None)
        if at is not None:
            tasks.append((at, number, task))
        elif number == 99:
            tasks = [(0.0, 4, side()), (0.0, 5, prepare())]
            for h in range(2):
                tasks.append((0.0, 20 + h, backward(h)))
                for s in range(2):
                    tasks.append((0.0, 2 * h + s, forward(h, s)))
                    tasks.append((0.0, 10 + 2 * h + s, update(h, s)))
    for copy in sends:
        copy.wait_send()


def store(out_in, res_in, out, res, sem):
    copies = [
        pltpu.make_async_copy(out_in, out, sem.at[0]),
        pltpu.make_async_copy(res_in, res, sem.at[1]),
    ]
    for copy in copies:
        copy.start()
    for copy in copies:
        copy.wait()


def body(observed, slip, green_left, green_right, block_ranks, neighbours):
    vmem, dma = pltpu.VMEM, pltpu.SemaphoreType.DMA
    hbm = pl.BlockSpec(memory_space=pltpu.HBM)
    whole = pl.BlockSpec(memory_space=pltpu.VMEM)
    shapes = (
        jax.ShapeDtypeStruct((2048, 256), F32),
        jax.ShapeDtypeStruct((4096, 128), F32),
    )
    joined = pl.pallas_call(
        kernel,
        name="step",
        out_shape=tuple(vmem(shape.shape, F32) for shape in shapes),
        in_specs=[hbm, hbm, hbm, hbm, pl.BlockSpec(memory_space=pltpu.SMEM), hbm],
        out_specs=(whole, whole),
        scratch_shapes=[
            vmem((2048 + 2 * HALO, 256), F32),
            vmem((4096, 128), BF16),
            vmem((2048, 256), BF16),
            vmem((2, 2, 64, 128), F32),
            vmem((8, 128), jnp.int32),
            vmem((2048, 128), F32),
            vmem((2048, 128), F32),
            vmem((1024, 512), BF16),
            vmem((2048, 256), F32),
            vmem((3, 512, 256), F32),
            vmem((512, 1024), BF16),
            vmem((2, 256, 128), BF16),
            vmem((2, 2, 512, 128), F32),
            vmem((2, 2, 512, 128), F32),
            vmem((2, 2, 512, 128), F32),
            vmem((2, 2, 2, 64, 128), F32),
            vmem((2, 2, 64, 128), F32),
            vmem((2, 2, 2, 64, 128), F32),
            vmem((2, 2, 3, 64, 128), F32),
            vmem((2, 2, 64, 128), F32),
            vmem((2, 2, 1024, 128), F32),
            vmem((2, 64, 128), F32),
            vmem((2, 64, 128), F32),
            vmem((2, 4, 64, 128), F32),
            vmem((2, 1024, 128), BF16),
            vmem((2, 2, 256, 128), F32),
            vmem((2, 2, 2, 32, 128), F32),
            vmem((2, 2, 2, 2, 32, 128), F32),
            vmem((2, 2, 2, 32, 128), F32),
            vmem((2, 128, 128), F32),
            vmem((2, 2048, 128), F32),
            dma((N_SEM,)),
            dma((N_SEM,)),
            dma((32,)),
        ],
        compiler_params=pltpu.CompilerParams(
            collective_id=0, has_side_effects=True, vmem_limit_bytes=40 * 2**20
        ),
        cost_estimate=pl.CostEstimate(flops=10**9, bytes_accessed=12 * 2**20, transcendentals=0),
    )(*(pltpu.with_memory_space_constraint(value, pltpu.HBM) for value in (observed, slip, green_left, green_right)), block_ranks, pltpu.with_memory_space_constraint(neighbours.T, pltpu.HBM))
    return pl.pallas_call(
        store,
        name="store",
        out_shape=shapes,
        in_specs=[whole, whole],
        out_specs=(hbm, hbm),
        scratch_shapes=[dma((2,))],
        compiler_params=pltpu.CompilerParams(vmem_limit_bytes=4 * 2**20),
    )(*(pltpu.with_memory_space_constraint(value, pltpu.VMEM) for value in joined))


def solution(mesh):
    return jax.shard_map(
        body,
        mesh=mesh,
        in_specs=(
            P("row", None),
            P("col", None),
            P("row", "col"),
            P("col", "row"),
            P("row", "col"),
            P("col", None),
        ),
        out_specs=(P("col", None), P("row", None)),
        check_vma=False,
    )
```

time: 83.6 us -> 76.5 us (0.915)
  Pallas kernels: 79.6 us -> 74.3 us
  local copies, waits for them, and re-layouts: 2.64 us -> 0 us
    pallas_call x1, Pallas kernels: 75.4 us -> 72.3 us  [body(): pl.pallas_call(kernel, name='step', out_shape=tuple((vmem(shape.shape, F3...]
    unnamed x4 -> x0, local copies, waits for them, and re-layouts: 2.64 us -> none
    pallas_call x1, Pallas kernels: 4.25 us -> 2.03 us  [body(): pl.pallas_call(store, name='store', out_shape=shapes, in_specs=[whole, wh...]
where the time goes in v3:
time: 76.5 us; the launch traced here: 75.6 us
  Pallas kernels  74.3 us (97%)
  between operations  1.29 us (2%)
    pallas_call x1, Pallas kernels, body(): pl.pallas_call(kernel, name='step', out_shape=tuple((vmem(shape.shape, F3...  72.3 us
    pallas_call x1, Pallas kernels, body(): pl.pallas_call(store, name='store', out_shape=shapes, in_specs=[whole, wh...  2.03 us

profile of v3, /device:TPU:2, one launch (start us, length us, event | category | flops | bytes accessed | tf_op | source)
XLA Modules:
  0.0 75.6 jit_solution(13367739831620224171)
XLA Ops:
  1.3 72.3 %step.1 = (f32[2048,256]{1,0:T(8,128)S(1)}, f32[4096,128]{1,0:T(8,128)S(1)}) custom-call(f32[4096,128]{1,0:T(8,128)} %obs.1, f32[2048,256]{1,0:T(8,128)} %slip.1, bf16[4096,128]{1,0:T(8,128)(2,1)} %gl.1, bf16[2048,256]{1,0:T(8,128)(2,1)} %gr.1, s32[1,1]{1,0:T(1,128)S(6)} %copy.8.rank, s32[8,2048]{1,0:T(8,128)} %bitcast.1), custom_call_target="tpu_custom_call" | custom-call | flops 1000000000 | bytes 12582912 | tf_op jit(solution)/shard_map/step/pallas_call | solution.py:516
  73.6 2.0 %store.1 = (f32[2048,256]{1,0:T(8,128)}, f32[4096,128]{1,0:T(8,128)}) custom-call(f32[2048,256]{1,0:T(8,128)S(1)} %get-tuple-element.4.out_in, f32[4096,128]{1,0:T(8,128)S(1)} %get-tuple-element.5.res_in), custom_call_target="tpu_custom_call" | custom-call | tf_op jit(solution)/shard_map/store/pallas_call | solution.py:563

commit v4 on v3

--- a/solution.py
+++ b/solution.py
@@ -10,8 +10,9 @@
 BF16 = jnp.bfloat16
 HALO = 64
 N_SEM = 240
-LAG_FORWARD, LAG_BACK = 3.5, 5.0
-FAR_OVER_Z = ((0, 0), (0, 1), (1, 0), (1, 1))
+SUM_Z_FIRST, GATHER_Z_LAST = (), (1,)
+LAG_FORWARD, LAG_BACK = 3.5, 4.2
+FAR_OVER_Z = ((1, 0), (1, 1))
 
 
 def lane_low(shape):
@@ -105,8 +106,14 @@
     keep_lane = lax.broadcasted_iota(jnp.int32, (256, 128), 1) < rank[0, 0]
     early = {}
 
-    def x_block(at):
-        return ds(((x + at) % 4) * 512, 512, 512)
+    def share_right(s, first, size):
+        def rows(at):
+            return ds(((x + at) % 4) * 256 + first, size, 64)
+
+        return [
+            send(grsend.at[s, rows(at)], grrecv.at[slot, s, pl.ds(first, size)], to)
+            for slot, at, to in ((1, 2, x_far), (0, 3, x_prev), (2, 1, x_next))
+        ]
 
     def product(half, h, s):
         first = half * 2048 + s * 512
@@ -138,11 +145,12 @@
             for s in range(2):
                 psend[h, s] = product(1, h, s)
         def widen_right(i, carry):
-            rows = ds(i * 256, 256, 256)
-            grsend[rows, :] = grv[rows, :].astype(F32)
+            for piece in range(2):
+                rows = ds(i * 128 + piece * 64, 64, 64)
+                grsend[piece, ds(i * 64, 64, 64), :] = grv[rows, :].astype(F32)
             return carry
 
-        lax.fori_loop(0, 8, widen_right, 0)
+        lax.fori_loop(0, 16, widen_right, 0)
         yield -9.0
         pl.semaphore_wait(barrier, len(partners))
         for h in range(2):
@@ -151,11 +159,8 @@
                     send(psend.at[h, s, pl.ds(i * 128, 128)], precv.at[h, s, pl.ds(i * 128, 128)], sibling)
                     for i in range(4)
                 ]
-        early["gr"] = [
-            send(grsend.at[x_block(3)], grrecv.at[0], x_prev),
-            send(grsend.at[x_block(2)], grrecv.at[1], x_far),
-            send(grsend.at[x_block(1)], grrecv.at[2], x_next),
-        ]
+        early["gr", 0] = share_right(0, 0, 256)
+        early["gr", 1] = share_right(1, 0, 256)
         yield -8.0
         load_gl[1].wait()
         for h in range(2):
@@ -217,19 +222,33 @@
             return ds(((y + at) % 4) * 128 + sub * 64, 64, 64)
 
         other = 1 - zl
-        pair1 = send(values.at[part(2, other)], azr.at[h, s, 0], z_pair)
-        up1 = send(values.at[part(1, other)], ay.at[h, s, 0], y_next)
-        down1 = send(values.at[part(3, other)], ay.at[h, s, 1], y_prev)
-        up2 = send(values.at[part(1, zl)], af.at[h, s, 0], y_next)
-        down2 = send(values.at[part(3, zl)], af.at[h, s, 1], y_prev)
-        yield 3.0 + lag
-        up1.wait_recv()
-        down1.wait_recv()
-        azs[h, s] = values[part(0, other), :] + ay[h, s, 0] + ay[h, s, 1]
-        pair2 = send(azs.at[h, s], azr.at[h, s, 1], z_pair)
-        pair1.wait_recv()
-        afs[h, s] = values[part(2, zl), :] + azr[h, s, 0]
-        far = send(afs.at[h, s], af.at[h, s, 2], y_far)
+        z_first = h in SUM_Z_FIRST
+        if z_first:
+            pairs = [send(values.at[part(at, other)], azr.at[h, s, at], z_pair) for at in (2, 1, 3, 0)]
+            yield 3.6 + lag
+            for copy in pairs:
+                copy.wait_recv()
+            for slot, at in enumerate((1, 3, 2)):
+                afs[h, s, slot] = values[part(at, zl), :] + azr[h, s, at]
+            far = send(afs.at[h, s, 2], af.at[h, s, 2], y_far)
+            up2 = send(afs.at[h, s, 0], af.at[h, s, 0], y_next)
+            down2 = send(afs.at[h, s, 1], af.at[h, s, 1], y_prev)
+            arrive = (far, up2, down2)
+        else:
+            pair1 = send(values.at[part(2, other)], azr.at[h, s, 1], z_pair)
+            up1 = send(values.at[part(1, other)], ay.at[h, s, 0], y_next)
+            down1 = send(values.at[part(3, other)], ay.at[h, s, 1], y_prev)
+            up2 = send(values.at[part(1, zl)], af.at[h, s, 0], y_next)
+            down2 = send(values.at[part(3, zl)], af.at[h, s, 1], y_prev)
+            yield 3.0 + lag
+            up1.wait_recv()
+            down1.wait_recv()
+            azs[h, s] = values[part(0, other), :] + ay[h, s, 0] + ay[h, s, 1]
+            pair2 = send(azs.at[h, s], azr.at[h, s, 0], z_pair)
+            pair1.wait_recv()
+            afs[h, s, 2] = values[part(2, zl), :] + azr[h, s, 1]
+            far = send(afs.at[h, s, 2], af.at[h, s, 2], y_far)
+            arrive = (up2, down2, pair2, far)
         top, bottom = obsv[0, s], obsv[1, s]
         low = lane_low((64, 128))
         if h == 0:
@@ -240,9 +259,9 @@
         mine = residual.at[part(0, zl)]
         mine[...] = values[part(0, zl), :] - seen
         yield 6.8 + lag
-        for copy in (up2, down2, pair2, far):
+        for copy in arrive:
             copy.wait_recv()
-        mine[...] = mine[...] + af[h, s, 0] + af[h, s, 1] + af[h, s, 2] + azr[h, s, 1]
+        mine[...] = mine[...] + af[h, s, 0] + af[h, s, 1] + af[h, s, 2] + azr[h, s, 0]
 
         def share(at, sub, to):
             shard = residual.at[part(at, sub)]
@@ -253,14 +272,22 @@
         up1 = share(0, zl, y_next)
         down1 = share(0, zl, y_prev)
         yield 9.9 + lag
-        pair1.wait_recv()
-        up2 = share(0, other, y_next)
-        down2 = share(0, other, y_prev)
-        yield 10.4 + lag
-        far.wait_recv()
-        pair2 = share(2, zl, z_pair)
+        if h in GATHER_Z_LAST:
+            yield 10.4 + lag
+            far.wait_recv()
+            rest = [pair1, share(2, zl, z_pair)]
+            up1.wait_recv()
+            rest.append(share(3, zl, z_pair))
+            down1.wait_recv()
+            rest.append(share(1, zl, z_pair))
+        else:
+            pair1.wait_recv()
+            rest = [up1, down1, share(0, other, y_next), share(0, other, y_prev)]
+            yield 10.4 + lag
+            far.wait_recv()
+            rest.append(share(2, zl, z_pair))
         yield 13.6 + lag
-        for copy in (up1, down1, up2, down2, pair2):
+        for copy in rest:
             copy.wait_recv()
 
     def backward(h):
@@ -298,7 +325,7 @@
 
     def update(h, s):
         lag = LAG_BACK * h + 0.8 * s
-        yield 19.7 + LAG_BACK * h + 0.01 * s
+        yield 19.7 + LAG_BACK * h + (0.2, 0.01)[h] * s
         part_grad = grad.at[h, s]
         part_grad[...] = jnp.dot(grcat[pl.ds(s * 256, 256), :], bd[h], preferred_element_type=F32)
 
@@ -368,9 +395,9 @@
         yield 32.2 + lag
         z_up1.wait_recv()
         z_up2 = spread(0, 3, 0, 32, zh_next)
+        send_x(3)
         z_down1.wait_recv()
         z_down2 = spread(0, 1, 32, 32, zh_prev)
-        send_x(3)
         send_x(1)
         merge(0, 3)
         merge(0, 1)
@@ -462,13 +489,12 @@
             for s in range(2):
                 rows = ds((x * 4 + shard) * 128 + s * 64, 64, 64)
                 grcat[pl.ds(s * 256 + shard * 64, 64), pl.ds(0, 256)] = grv[rows, :]
-        yield 16.4
-        for d in range(1, 4):
-            early["gr"][d - 1].wait_recv()
-            for shard in range(4):
-                for s in range(2):
-                    rows = pl.ds(shard * 128 + s * 64, 64)
-                    grcat[pl.ds(s * 256 + shard * 64, 64), pl.ds(d * 256, 256)] = grrecv[d - 1, rows, :].astype(BF16)
+        for s in range(2):
+            yield (13.7, 19.8)[s]
+            for copy in early["gr", s]:
+                copy.wait_recv()
+            for d in range(1, 4):
+                grcat[pl.ds(s * 256, 256), pl.ds(d * 256, 256)] = grrecv[d - 1, s].astype(BF16)
         yield 24.8
         join_res(0)
         yield 30.0
@@ -528,18 +554,18 @@
             vmem((2048, 128), F32),
             vmem((2048, 128), F32),
             vmem((1024, 512), BF16),
-            vmem((2048, 256), F32),
-            vmem((3, 512, 256), F32),
+            vmem((2, 1024, 256), F32),
+            vmem((3, 2, 256, 256), F32),
             vmem((512, 1024), BF16),
             vmem((2, 256, 128), BF16),
             vmem((2, 2, 512, 128), F32),
             vmem((2, 2, 512, 128), F32),
             vmem((2, 2, 512, 128), F32),
-            vmem((2, 2, 2, 64, 128), F32),
+            vmem((2, 2, 4, 64, 128), F32),
             vmem((2, 2, 64, 128), F32),
             vmem((2, 2, 2, 64, 128), F32),
             vmem((2, 2, 3, 64, 128), F32),
-            vmem((2, 2, 64, 128), F32),
+            vmem((2, 2, 3, 64, 128), F32),
             vmem((2, 2, 1024, 128), F32),
             vmem((2, 64, 128), F32),
             vmem((2, 64, 128), F32),

time: 76.5 us -> 75.9 us (level)
  no operation moved by 1% of the time
where the time goes in v4:
time: 75.9 us; the launch traced here: 75.6 us
  Pallas kernels  74.3 us (98%)
  between operations  1.29 us (2%)
    pallas_call x1, Pallas kernels, body(): pl.pallas_call(kernel, name='step', out_shape=tuple((vmem(shape.shape, F3...  72.2 us
    pallas_call x1, Pallas kernels, body(): pl.pallas_call(store, name='store', out_shape=shapes, in_specs=[whole, wh...  2.03 us

profile of v4, /device:TPU:2, one launch (start us, length us, event | category | flops | bytes accessed | tf_op | source)
XLA Modules:
  0.0 75.6 jit_solution(9322525604865732914)
XLA Ops:
  1.3 72.2 %step.1 = (f32[2048,256]{1,0:T(8,128)S(1)}, f32[4096,128]{1,0:T(8,128)S(1)}) custom-call(f32[4096,128]{1,0:T(8,128)} %obs.1, f32[2048,256]{1,0:T(8,128)} %slip.1, bf16[4096,128]{1,0:T(8,128)(2,1)} %gl.1, bf16[2048,256]{1,0:T(8,128)(2,1)} %gr.1, s32[1,1]{1,0:T(1,128)S(6)} %copy.8.rank, s32[8,2048]{1,0:T(8,128)} %bitcast.1), custom_call_target="tpu_custom_call" | custom-call | flops 1000000000 | bytes 12582912 | tf_op jit(solution)/shard_map/step/pallas_call | solution.py:542
  73.5 2.0 %store.1 = (f32[2048,256]{1,0:T(8,128)}, f32[4096,128]{1,0:T(8,128)}) custom-call(f32[2048,256]{1,0:T(8,128)S(1)} %get-tuple-element.4.out_in, f32[4096,128]{1,0:T(8,128)S(1)} %get-tuple-element.5.res_in), custom_call_target="tpu_custom_call" | custom-call | tf_op jit(solution)/shard_map/store/pallas_call | solution.py:589

commit v5 on v4

--- a/solution.py
+++ b/solution.py
@@ -141,9 +141,20 @@
         rhs[1, pl.ds(0, 128), :] = jnp.where(low, turned, 0.0).astype(BF16)
         rhs[1, pl.ds(128, 128), :] = jnp.where(low, 0.0, inner).astype(BF16)
         load_gl[0].wait()
-        for h in range(2):
+        for s in range(2):
+            psend[0, s] = product(1, 0, s)
+
+        def swap_products(h):
             for s in range(2):
-                psend[h, s] = product(1, h, s)
+                early["pred", h, s] = [
+                    send(psend.at[h, s, pl.ds(i * 128, 128)], precv.at[h, s, pl.ds(i * 128, 128)], sibling)
+                    for i in range(4)
+                ]
+
+        yield -9.0
+        pl.semaphore_wait(barrier, len(partners))
+        swap_products(0)
+
         def widen_right(i, carry):
             for piece in range(2):
                 rows = ds(i * 128 + piece * 64, 64, 64)
@@ -151,16 +162,11 @@
             return carry
 
         lax.fori_loop(0, 16, widen_right, 0)
-        yield -9.0
-        pl.semaphore_wait(barrier, len(partners))
-        for h in range(2):
-            for s in range(2):
-                early["pred", h, s] = [
-                    send(psend.at[h, s, pl.ds(i * 128, 128)], precv.at[h, s, pl.ds(i * 128, 128)], sibling)
-                    for i in range(4)
-                ]
         early["gr", 0] = share_right(0, 0, 256)
         early["gr", 1] = share_right(1, 0, 256)
+        for s in range(2):
+            psend[1, s] = product(1, 1, s)
+        swap_products(1)
         yield -8.0
         load_gl[1].wait()
         for h in range(2):

time: 75.9 us -> 76.6 us (level)
  no operation moved by 1% of the time
where the time goes in v5:
time: 76.6 us; the launch traced here: 76.1 us
  Pallas kernels  74.8 us (98%)
  between operations  1.29 us (2%)
    pallas_call x1, Pallas kernels, body(): pl.pallas_call(kernel, name='step', out_shape=tuple((vmem(shape.shape, F3...  72.8 us
    pallas_call x1, Pallas kernels, body(): pl.pallas_call(store, name='store', out_shape=shapes, in_specs=[whole, wh...  2.03 us

profile of v5, /device:TPU:2, one launch (start us, length us, event | category | flops | bytes accessed | tf_op | source)
XLA Modules:
  0.0 76.1 jit_solution(9159453957967618999)
XLA Ops:
  1.3 72.8 %step.1 = (f32[2048,256]{1,0:T(8,128)S(1)}, f32[4096,128]{1,0:T(8,128)S(1)}) custom-call(f32[4096,128]{1,0:T(8,128)} %obs.1, f32[2048,256]{1,0:T(8,128)} %slip.1, bf16[4096,128]{1,0:T(8,128)(2,1)} %gl.1, bf16[2048,256]{1,0:T(8,128)(2,1)} %gr.1, s32[1,1]{1,0:T(1,128)S(6)} %copy.8.rank, s32[8,2048]{1,0:T(8,128)} %bitcast.1), custom_call_target="tpu_custom_call" | custom-call | flops 1000000000 | bytes 12582912 | tf_op jit(solution)/shard_map/step/pallas_call | solution.py:548
  74.1 2.0 %store.1 = (f32[2048,256]{1,0:T(8,128)}, f32[4096,128]{1,0:T(8,128)}) custom-call(f32[2048,256]{1,0:T(8,128)S(1)} %get-tuple-element.4.out_in, f32[4096,128]{1,0:T(8,128)S(1)} %get-tuple-element.5.res_in), custom_call_target="tpu_custom_call" | custom-call | tf_op jit(solution)/shard_map/store/pallas_call | solution.py:595
